TPU v7x, 128 devices: a whole 4x4x4 slice. The times are simulated.
128 devices in a mesh: ctx: 32 (over z, x, core), hg: 4 (over y).
Axes of the slice: x: 4, y: 4, z: 4, core: 2. Of those that a mesh axis runs over, the one named last changes fastest.
Arguments:
- queries: bfloat16 [8192, 8, 8, 128], P('ctx', 'hg'), may hold values from -6 to 6
- key_vectors: bfloat16 [8192, 8, 128], P('ctx', 'hg'), may hold values from -6 to 6
- value_vectors: bfloat16 [8192, 8, 128], P('ctx', 'hg'), may hold values from -6 to 6
- outputs: bfloat16 [8192, 8, 8, 128], P('ctx', 'hg'), may hold values from -1.796875 to 1.796875
- out_grads: bfloat16 [8192, 8, 8, 128], P('ctx', 'hg'), may hold values from -18 to 18
- log_sums: bfloat16 [8192, 8, 8], P('ctx', 'hg'), may hold values from -0.5 to 14
- head_kind: int32 [8], replicated, may hold values from 0 to 1, as said below
- sink_len: int32 [8], replicated, may hold values from 64 to 128, as said below
- window_len: int32 [8], replicated, may hold values from 128 to 256, as said below
Outputs:
- query_grads: bfloat16 [8192, 8, 8, 128], P('ctx', 'hg')
- key_grads: bfloat16 [8192, 8, 128], P('ctx', 'hg')
- value_grads: bfloat16 [8192, 8, 128], P('ctx', 'hg')
Inputs may be any that keep to these rules, and one draw needn't show every extreme that they name: `head_kind`: among KV heads 4m to 4m + 3 exactly two have 1. In every draw some such four hold both of their 1s in heads 4m, 4m + 1 or both in 4m + 2, 4m + 3. `sink_len`: some KV head with head_kind 0 has exactly 128. `window_len`: some KV head with head_kind 0 has exactly 256.
All inputs are finite; a program needn't handle non-finite values.
Results may differ from a plain program's by a relative error of at most 0.005.
Values may be sent and summed in bfloat16 or wider, within the bound.
A program may use at most 64 MiB of HBM per device.

v0:
```python
import jax
import jax.numpy as jnp
from jax import lax
from jax.sharding import PartitionSpec as P

SINK_MAX = 128
WIN_MAX = 256


def from_partner(value, axis, distance):
    mask = 2**distance
    pairs = [(source, source ^ mask) for source in range(lax.axis_size(axis))]
    return lax.ppermute(value, axis, pairs)


def from_behind(block, axis, distance):
    devices = range(lax.axis_size(axis))
    route = [(i - distance, i) for i in devices if i - distance in devices]
    return lax.ppermute(block, axis, route)


def spread(value, axis, source):
    kept = jnp.where(lax.axis_index(axis) == source, value, 0).astype(value.dtype)
    return lax.psum(kept, axis)


def block_grads(
    query_vecs, grad_vecs, lse_vecs, total_vecs, key_block, value_block, allowed, scaling
):
    scores = (
        jnp.einsum("qd,kd->qk", query_vecs, key_block, preferred_element_type=jnp.float32) * scaling
    )
    weights = jnp.where(allowed, jnp.exp(scores - lse_vecs[:, None]), 0.0)
    weights_low = weights.astype(jnp.bfloat16)
    value_part = jnp.einsum("qk,qd->kd", weights_low, grad_vecs, preferred_element_type=jnp.float32)
    weight_grad = jnp.einsum(
        "qd,kd->qk", grad_vecs, value_block, preferred_element_type=jnp.float32
    )
    score_grad = (weights * (weight_grad - total_vecs[:, None])).astype(jnp.bfloat16)
    query_part = jnp.einsum("qk,kd->qd", score_grad, key_block, preferred_element_type=jnp.float32)
    key_part = jnp.einsum("qk,qd->kd", score_grad, query_vecs, preferred_element_type=jnp.float32)
    return (query_part, key_part, value_part)


def row_totals(grad_rows, out_rows):
    return jnp.sum(grad_rows.astype(jnp.float32) * out_rows.astype(jnp.float32), axis=-1)


def causal_pass(
    query_vecs,
    grad_vecs,
    lse_vecs,
    total_vecs,
    positions,
    key_all,
    value_all,
    block_count,
    width,
    scaling,
    key_sum,
    value_sum,
):

    def advance(block_index, state):
        query_acc, key_acc, value_acc = state
        start = block_index * width
        key_block = lax.dynamic_slice_in_dim(key_all, start, width, 0)
        value_block = lax.dynamic_slice_in_dim(value_all, start, width, 0)
        key_pos = start + lax.iota(jnp.int32, width)
        allowed = key_pos[None, :] <= positions[:, None]
        query_part, key_part, value_part = block_grads(
            query_vecs, grad_vecs, lse_vecs, total_vecs, key_block, value_block, allowed, scaling
        )
        key_acc = lax.dynamic_update_slice_in_dim(
            key_acc, lax.dynamic_slice_in_dim(key_acc, start, width, 0) + key_part, start, 0
        )
        value_acc = lax.dynamic_update_slice_in_dim(
            value_acc, lax.dynamic_slice_in_dim(value_acc, start, width, 0) + value_part, start, 0
        )
        return (query_acc + query_part, key_acc, value_acc)

    start_state = (jnp.zeros(query_vecs.shape, jnp.float32), key_sum, value_sum)
    return lax.fori_loop(0, block_count, advance, start_state)


def shards(
    queries,
    key_vectors,
    value_vectors,
    outputs,
    out_grads,
    log_sums,
    head_kind,
    sink_len,
    window_len,
):
    tok_rows = queries.shape[0]
    per_head = queries.shape[2]
    head_dim = queries.shape[3]
    ctx_count = lax.axis_size("ctx")
    ctx_pos = lax.axis_index("ctx")
    group = lax.axis_index("hg")
    scaling = head_dim ** (-0.5)
    seq_len = tok_rows * ctx_count
    width = seq_len // 8
    vec_count = tok_rows * per_head
    base_id = 2 * group
    partner_id = 2 * jnp.bitwise_xor(group, 1) + 1
    first_ret = head_kind[base_id] == 1
    local_pair = head_kind[base_id] + head_kind[base_id + 1] == 1
    other_id = jnp.where(local_pair, base_id + 1, partner_id)
    stream_id = jnp.where(first_ret, other_id, base_id)
    first_set = (
        queries[:, 0],
        key_vectors[:, 0],
        value_vectors[:, 0],
        outputs[:, 0],
        out_grads[:, 0],
        log_sums[:, 0],
    )
    second_set = (
        queries[:, 1],
        key_vectors[:, 1],
        value_vectors[:, 1],
        outputs[:, 1],
        out_grads[:, 1],
        log_sums[:, 1],
    )
    spare_set = from_partner(
        (
            queries[:, 1],
            key_vectors[:, 1],
            value_vectors[:, 1],
            outputs[:, 1],
            out_grads[:, 1],
            log_sums[:, 1],
        ),
        "hg",
        0,
    )
    other_set = jax.tree.map(
        lambda mine_part, their_part: jnp.where(local_pair, mine_part, their_part),
        second_set,
        spare_set,
    )
    full_query, full_keys, full_values, full_outputs, full_grads, full_logsums = jax.tree.map(
        lambda first_part, other_part: jnp.where(first_ret, first_part, other_part),
        first_set,
        other_set,
    )
    band_query, band_keys, band_values, band_outputs, band_grads, band_logsums = jax.tree.map(
        lambda first_part, other_part: jnp.where(first_ret, other_part, first_part),
        first_set,
        other_set,
    )
    vec_rows = lax.iota(jnp.int32, vec_count) // per_head
    query_vecs = full_query.reshape(vec_count, head_dim)
    grad_vecs = full_grads.reshape(vec_count, head_dim)
    total_vecs = row_totals(full_grads, full_outputs).reshape(vec_count)
    lse_vecs = full_logsums.reshape(vec_count).astype(jnp.float32)
    positions = ctx_pos * tok_rows + vec_rows
    all_keys, all_values = (
        lax.all_gather(full_keys, "ctx", axis=0, tiled=True),
        lax.all_gather(full_values, "ctx", axis=0, tiled=True),
    )
    zero_sum = jnp.zeros((seq_len, head_dim), jnp.float32)
    block_count = ((ctx_pos + 1) * tok_rows + width - 1) // width
    query_acc, key_sum, value_sum = causal_pass(
        query_vecs,
        grad_vecs,
        lse_vecs,
        total_vecs,
        positions,
        all_keys,
        all_values,
        block_count,
        width,
        scaling,
        zero_sum,
        zero_sum,
    )
    key_home, value_home = (
        lax.psum_scatter(key_sum, "ctx", scatter_dimension=0, tiled=True),
        lax.psum_scatter(value_sum, "ctx", scatter_dimension=0, tiled=True),
    )
    held_dq = (query_acc * scaling).astype(jnp.bfloat16).reshape(tok_rows, per_head, head_dim)
    full_dk = (key_home * scaling).astype(jnp.bfloat16)
    full_dv = value_home.astype(jnp.bfloat16)
    sink_count = sink_len[stream_id]
    window = window_len[stream_id]
    halo_keys, halo_values = from_behind((band_keys, band_values), "ctx", 1)
    sink_keys, sink_values = (
        spread(band_keys[:SINK_MAX], "ctx", 0),
        spread(band_values[:SINK_MAX], "ctx", 0),
    )
    key_block = jnp.concatenate([sink_keys, halo_keys, band_keys], axis=0)
    value_block = jnp.concatenate([sink_values, halo_values, band_values], axis=0)
    first_row = ctx_pos * tok_rows
    key_pos = jnp.concatenate(
        [
            lax.iota(jnp.int32, SINK_MAX),
            first_row - WIN_MAX + lax.iota(jnp.int32, WIN_MAX),
            first_row + lax.iota(jnp.int32, tok_rows),
        ]
    )
    positions_band = first_row + vec_rows
    distance = positions_band[:, None] - key_pos[None, :]
    in_sink = lax.iota(jnp.int32, SINK_MAX + WIN_MAX + tok_rows) < SINK_MAX
    allowed = jnp.where(
        in_sink[None, :],
        (key_pos < sink_count)[None, :] & (distance >= window),
        (key_pos >= 0)[None, :] & (distance >= 0) & (distance < window),
    )
    query_part, key_part, value_part = block_grads(
        band_query.reshape(vec_count, head_dim),
        band_grads.reshape(vec_count, head_dim),
        band_logsums.reshape(vec_count).astype(jnp.float32),
        row_totals(band_grads, band_outputs).reshape(vec_count),
        key_block,
        value_block,
        allowed,
        scaling,
    )
    sink_key_sum, sink_value_sum = lax.psum((key_part[:SINK_MAX], value_part[:SINK_MAX]), "ctx")
    band_start = SINK_MAX + WIN_MAX
    back_keys, back_values = from_behind(
        (key_part[SINK_MAX:band_start], value_part[SINK_MAX:band_start]), "ctx", -1
    )
    at_root = ctx_pos == 0
    own_keys = (
        key_part[band_start:]
        .at[tok_rows - WIN_MAX :]
        .add(back_keys)
        .at[:SINK_MAX]
        .add(jnp.where(at_root, sink_key_sum, 0.0))
    )
    own_values = (
        value_part[band_start:]
        .at[tok_rows - WIN_MAX :]
        .add(back_values)
        .at[:SINK_MAX]
        .add(jnp.where(at_root, sink_value_sum, 0.0))
    )
    band_dq = (query_part * scaling).astype(jnp.bfloat16).reshape(tok_rows, per_head, head_dim)
    band_dk = (own_keys * scaling).astype(jnp.bfloat16)
    band_dv = own_values.astype(jnp.bfloat16)
    full_set = (held_dq, full_dk, full_dv)
    band_set = (band_dq, band_dk, band_dv)
    away_set = jax.tree.map(
        lambda full_part, band_part: jnp.where(first_ret, band_part, full_part), full_set, band_set
    )
    home_set = from_partner((away_set[0], away_set[1], away_set[2]), "hg", 0)
    first_out = jax.tree.map(
        lambda full_part, band_part: jnp.where(first_ret, full_part, band_part), full_set, band_set
    )
    second_out = jax.tree.map(
        lambda away_part, home_part: jnp.where(local_pair, away_part, home_part), away_set, home_set
    )
    return tuple(
        (
            jnp.stack([first_part, second_part], axis=1)
            for first_part, second_part in zip(first_out, second_out)
        )
    )


def solution(mesh):
    return jax.shard_map(
        shards,
        mesh=mesh,
        in_specs=(
            P("ctx", "hg", None, None),
            P("ctx", "hg", None),
            P("ctx", "hg", None),
            P("ctx", "hg", None, None),
            P("ctx", "hg", None, None),
            P("ctx", "hg", None),
            P(),
            P(),
            P(),
        ),
        out_specs=(P("ctx", "hg", None, None), P("ctx", "hg", None), P("ctx", "hg", None)),
        check_vma=False,
    )
```

profile of v0, /device:TPU:0, one launch (start us, length us, event | category | flops | bytes accessed | tf_op | source)
XLA Modules:
  0.0 515.0 jit_solution(5731998508755547654)
XLA Ops:
  7.3 1.3 fusion.55
  8.6 1.7 collective-permute-start
  10.4 1.2 fusion.54
  12.0 1.3 fusion.56
  17.9 0.7 all-gather.3.cloned.1.call-update
  18.7 1.1 slice_bitcast_fusion.2
  19.7 1.7 collective-permute-start.1
  21.6 0.7 slice_bitcast_fusion.3
  22.6 1.9 slice_bitcast_fusion.1
  24.5 1.7 collective-permute-start.4
  26.1 0.8 slice_bitcast_fusion
  29.3 5.5 %collective-permute-done.2 = bf16[256,8]{0,1:T(8,128)(2,1)S(1)} collective-permute-done((bf16[256,8]{0,1:T(8,128)(2,1)S(1)}, bf16[256,8]{0,1:T(8,128)(2,1)S(1)}, u32[]{:S(2)}, u32[]{:S(2)}) %collective-permute-start.2) | collective-permute-done | bytes 4128 | tf_op jit(solution)/shard_map/ppermute | solution.py:13
  35.3 1.3 collective-permute-start.6
  36.6 4.8 collective-permute-start.7
  41.4 0.9 fusion.33
  42.3 73.9 %all-reduce.7.cloned.1.call-done = (bf16[128,128]{1,0:T(8,128)(2,1)}, bf16[128,128]{1,0:T(8,128)(2,1)}) async-done(((bf16[128,128]{1,0:T(8,128)(2,1)}, bf16[128,128]{1,0:T(8,128)(2,1)}), (bf16[128,128]{1,0:T(8,128)(2,1)}, bf16[128,128]{1,0:T(8,128)(2,1)})) %all-reduce.7.cloned.1.call-update) | async-done | bytes 65552 | tf_op jit(solution)/shard_map/psum | solution.py:24
  116.2 6.4 %exponential_select_fusion = f32[2048,640]{1,0:T(8,128)} fusion(bf16[2048,128]{1,0:T(8,128)(2,1)} %get-tuple-element.203, f32[2048]{0:T(1024)S(1)} %reshape.220, s32[]{:T(128)} %bitcast.17, s32[640]{0:T(1024)S(1)} %pad_add_fusion, s32[2048]{0:T(1024)S(1)} %fusion.44, pred[640]{0:T(1024)(128)(4,1)S(1)} %get-tuple-element.219, ...), kind=kOutput, calls=%fused_computation.33 | convolution fusion | flops 350453760 | bytes 5951876 | tf_op jit(solution)/shard_map/qd,kd->qk/dot_general | solution.py:31
  122.7 0.8 copy-done.4
  123.5 1.1 multiply_reduce_fusion.1
  124.8 3.6 multiply_convert_fusion
  128.5 0.9 fusion.57
  130.0 0.9 fusion.30
  131.7 30.5 %all-gather.3.cloned.1.call-done = bf16[8192,128]{1,0:T(8,128)(2,1)} async-done(((bf16[256,128]{1,0:T(8,128)(2,1)}), bf16[8192,128]{1,0:T(8,128)(2,1)}) %all-gather.3.cloned.1.call-update) | async-done | bytes 2097168 | tf_op jit(solution)/shard_map/all_gather | solution.py:163
  162.2 45.8 %all-gather.5.cloned.1.call-done = bf16[8192,128]{1,0:T(8,128)(2,1)} async-done(((bf16[256,128]{1,0:T(8,128)(2,1)}), bf16[8192,128]{1,0:T(8,128)(2,1)}) %all-gather.5.cloned.1.call-update) | async-done | bytes 2097168 | tf_op jit(solution)/shard_map/all_gather | solution.py:164
  208.0 2.2 broadcast_in_dim.42
  210.3 2.3 broadcast_in_dim.42.clone
  212.6 15.2 %while.22 = (s32[]{:T(128)}, f32[2048,128]{1,0:T(8,128)S(1)}, f32[8192,128]{1,0:T(8,128)}, f32[8192,128]{1,0:T(8,128)}, s32[]{:T(128)}, /*index=5*/bf16[8192,128...) while((s32[]{:T(128)}, f32[2048,128]{1,0:T(8,128)S(1)}, ...), condition=%wide.wide.region_2.3_spmd.clone, body=%wide.wide.region_1.2_spmd.clone.sunk | while | flops 2710064128 | bytes 44888300 | solution.py:83
  212.6 2.2 fusion.108
  214.8 3.7 fusion.110
  218.5 2.4 convolution_add_fusion.4
  220.8 3.1 fusion.111
  224.0 3.8 fusion.112
  228.4 1.3 collective-permute-start.11
  229.8 1.3 collective-permute-start.9
  231.7 3.5 select_bitcast_fusion.2
  235.2 1.5 collective-permute-start.8
  236.7 74.7 %all-reduce.5.cloned.1.call-done = (f32[128,128]{1,0:T(8,128)}, f32[128,128]{1,0:T(8,128)}) async-done(((f32[128,128]{1,0:T(8,128)}, f32[128,128]{1,0:T(8,128)}), (f32[128,128]{1,0:T(8,128)}, f32[128,128]{1,0:T(8,128)})) %all-reduce.5.cloned.1.call-update) | async-done | bytes 131088 | tf_op jit(solution)/shard_map/psum | solution.py:224
  311.4 0.9 fusion.42
  312.3 0.9 fusion.43
  313.2 102.7 %reduce-scatter.5.cloned.1.call-done = f32[256,128]{1,0:T(8,128)} async-done(((f32[8192,128]{1,0:T(8,128)}), f32[256,128]{1,0:T(8,128)}) %reduce-scatter.5.cloned.1.call-update) | async-done | bytes 131088 | tf_op jit(solution)/shard_map/reduce_scatter | solution.py:184
  415.9 0.9 select_bitcast_fusion.4
  416.8 1.5 collective-permute-start.12
  418.4 82.8 %reduce-scatter.3.cloned.1.call-done = f32[256,128]{1,0:T(8,128)} async-done(((f32[8192,128]{1,0:T(8,128)}), f32[256,128]{1,0:T(8,128)}) %reduce-scatter.3.cloned.1.call-update) | async-done | bytes 131088 | tf_op jit(solution)/shard_map/reduce_scatter | solution.py:183
  501.2 0.9 select_bitcast_fusion.6
  502.2 1.6 collective-permute-start.10
  503.7 2.2 pad_maximum_fusion
  506.6 0.8 copy.38
  507.4 0.8 copy.39
  (94 shorter events, 10.0 us)
Async XLA Ops:
  7.2 34.3 %copy-start.2 = (bf16[256,2,8,128]{3,2,1,0:T(8,128)(2,1)S(1)}, bf16[256,2,8,128]{3,2,1,0:T(8,128)(2,1)}, u32[]{:S(2)}) copy-start(bf16[256,2,8,128]{3,2,1,0:T(8,128)(2,1)} %param.23) | copy-start | bytes 3145732
  7.2 27.6 %copy-start.8 = (bf16[256,2,8]{0,2,1:T(8,128)(2,1)S(1)}, bf16[256,2,8]{0,2,1:T(8,128)(2,1)}, u32[]{:S(2)}) copy-start(bf16[256,2,8]{0,2,1:T(8,128)(2,1)} %param.28) | copy-start | bytes 24580
  7.2 18.9 %copy-start.3 = (bf16[256,2,8,128]{3,2,1,0:T(8,128)(2,1)S(1)}, bf16[256,2,8,128]{3,2,1,0:T(8,128)(2,1)}, u32[]{:S(2)}) copy-start(bf16[256,2,8,128]{3,2,1,0:T(8,128)(2,1)} %param.26) | copy-start | bytes 3145732
  7.2 20.2 %copy-start.12 = (s32[8]{0:T(128)S(1)}, s32[8]{0:T(128)}, u32[]{:S(2)}) copy-start(s32[8]{0:T(128)} %param.30) | copy-start | bytes 100
  7.2 21.4 %copy-start.13 = (s32[8]{0:T(128)S(1)}, s32[8]{0:T(128)}, u32[]{:S(2)}) copy-start(s32[8]{0:T(128)} %param.31) | copy-start | bytes 100
  7.2 109.0 %all-reduce.7.cloned.1.call-start = ((), (), s32[]{:S(2)}) async-start(), calls=%async_computation.7 | async-start | bytes 131072 | tf_op jit(solution)/shard_map/psum | solution.py:24
  8.6 6.7 %collective-permute-start = (bf16[256,128]{1,0:T(8,128)(2,1)S(1)}, bf16[256,128]{1,0:T(8,128)(2,1)S(1)}, u32[]{:S(2)}, u32[]{:S(2)}) collective-permute-start(bf16[256,128]{1,0:T(8,128)(2,1)S(1)} %bitcast.178), channel_id=1, source_target_pairs={{0,1},{1,0},{2,3},{3,2},{4,5},{5,4},{6,7},{7,6},{8,9},{9,8},{10,11... | collective-permute-start | bytes 196616 | tf_op jit(solution)/shard_map/ppermute | solution.py:13
  11.6 5.0 collective-permute-start.3
  17.9 144.3 %all-gather.3.cloned.1.call-start = ((), (), s32[]{:S(2)}) async-start(), calls=%async_computation.2 | async-start | bytes 2162688 | tf_op jit(solution)/shard_map/all_gather | solution.py:163
  18.6 189.4 %all-gather.5.cloned.1.call-start = ((), (), s32[]{:S(2)}) async-start(), calls=%async_computation.3 | async-start | bytes 2162688 | tf_op jit(solution)/shard_map/all_gather | solution.py:164
  19.7 21.7 %collective-permute-start.1 = (bf16[256,8,128]{2,1,0:T(8,128)(2,1)S(1)}, bf16[256,8,128]{2,1,0:T(8,128)(2,1)}, u32[]{:S(2)}, u32[]{:S(2)}) collective-permute-start(bf16[256,8,128]{2,1,0:T(8,128)(2,1)S(1)} %slice_bitcast_fusion.2), channel_id=1, source_target_pairs={{0,1},{1,0},{2,3},{3,2},{4,5},{5,4},{6,7},{7,6},{8,9},{9,8},{10,11... | collective-permute-start | bytes 1572872 | tf_op jit(solution)/shard_map/ppermute | solution.py:13
  21.5 289.9 %all-reduce.5.cloned.1.call-start = ((), (), s32[]{:S(2)}) async-start(), calls=%async_computation.6 | async-start | bytes 262144 | tf_op jit(solution)/shard_map/psum | solution.py:224
  22.2 12.5 %collective-permute-start.2 = (bf16[256,8]{0,1:T(8,128)(2,1)S(1)}, bf16[256,8]{0,1:T(8,128)(2,1)S(1)}, u32[]{:S(2)}, u32[]{:S(2)}) collective-permute-start(bf16[256,8]{0,1:T(8,128)(2,1)S(1)} %slice_bitcast_fusion.3), channel_id=1, source_target_pairs={{0,1},{1,0},{2,3},{3,2},{4,5},{5,4},{6,7},{7,6},{8,9},{9,8},{10,11... | collective-permute-start | bytes 12296 | tf_op jit(solution)/shard_map/ppermute | solution.py:13
  24.5 98.2 %collective-permute-start.4 = (bf16[256,8,128]{2,1,0:T(8,128)(2,1)}, bf16[256,8,128]{2,1,0:T(8,128)(2,1)S(1)}, u32[]{:S(2)}, u32[]{:S(2)}) collective-permute-start(bf16[256,8,128]{2,1,0:T(8,128)(2,1)} %slice_bitcast_fusion.1), channel_id=1, source_target_pairs={{0,1},{1,0},{2,3},{3,2},{4,5},{5,4},{6,7},{7,6},{8,9},{9,8},{10,11... | collective-permute-start | bytes 1572872 | tf_op jit(solution)/shard_map/ppermute | solution.py:13
  27.0 96.5 %collective-permute-start.5 = (bf16[256,8,128]{2,1,0:T(8,128)(2,1)}, bf16[256,8,128]{2,1,0:T(8,128)(2,1)}, u32[]{:S(2)}, u32[]{:S(2)}) collective-permute-start(bf16[256,8,128]{2,1,0:T(8,128)(2,1)} %slice_bitcast_fusion), channel_id=1, source_target_pairs={{0,1},{1,0},{2,3},{3,2},{4,5},{5,4},{6,7},{7,6},{8,9},{9,8},{10,11... | collective-permute-start | bytes 1572872 | tf_op jit(solution)/shard_map/ppermute | solution.py:13
  35.3 81.0 %collective-permute-start.6 = (bf16[256,128]{1,0:T(8,128)(2,1)S(1)}, bf16[256,128]{1,0:T(8,128)(2,1)S(1)}, u32[]{:S(2)}, u32[]{:S(2)}) collective-permute-start(bf16[256,128]{1,0:T(8,128)(2,1)S(1)} %get-tuple-element.211), channel_id=1, source_target_pairs={{0,4},{4,8},{8,12},{12,16},{16,20},{20,24},{24,28},{28,32},{32,36}... | collective-permute-start | bytes 196616 | tf_op jit(solution)/shard_map/ppermute | solution.py:19
  36.6 88.2 %collective-permute-start.7 = (bf16[256,128]{1,0:T(8,128)(2,1)S(1)}, bf16[256,128]{1,0:T(8,128)(2,1)}, u32[]{:S(2)}, u32[]{:S(2)}) collective-permute-start(bf16[256,128]{1,0:T(8,128)(2,1)S(1)} %get-tuple-element.209), channel_id=1, source_target_pairs={{0,4},{4,8},{8,12},{12,16},{16,20},{20,24},{24,28},{28,32},{32,36}... | collective-permute-start | bytes 196616 | tf_op jit(solution)/shard_map/ppermute | solution.py:19
  116.2 6.4 %copy-start.9 = (bf16[256,128]{1,0:T(8,128)(2,1)}, bf16[256,128]{1,0:T(8,128)(2,1)S(1)}, u32[]{:S(2)}) copy-start(bf16[256,128]{1,0:T(8,128)(2,1)S(1)} %collective-permute-done.6) | copy-start | bytes 196612
  116.2 7.2 %copy-start.1 = (bf16[256,2,8,128]{3,2,1,0:T(8,128)(2,1)S(1)}, bf16[256,2,8,128]{3,2,1,0:T(8,128)(2,1)}, u32[]{:S(2)}) copy-start(bf16[256,2,8,128]{3,2,1,0:T(8,128)(2,1)} %param.27) | copy-start | bytes 3145732
  122.7 0.8 copy-start.4
  124.6 3.9 copy-start.7
  124.8 5.2 %slice-start = ((s8[5242880]{0:T(1024)(128)(4,1)}), s8[4194304]{0:T(1024)(128)(4,1)S(1)}, s32[]{:S(2)}) async-start(s8[5242880]{0:T(1024)(128)(4,1)} %bitcast.175), calls=%async_computation.8 | async-start | bytes 8388608
  124.8 3.6 copy-start.6
  124.8 5.1 slice-start.1
  128.4 2.4 copy-start
  130.0 1.6 copy-start.5
  131.5 284.4 %reduce-scatter.5.cloned.1.call-start = ((), (), s32[]{:S(2)}) async-start(), calls=%async_computation.5 | async-start | bytes 4325376 | tf_op jit(solution)/shard_map/reduce_scatter | solution.py:184
  227.8 3.9 copy-start.10
  227.8 3.9 copy-start.11
  227.8 273.4 %reduce-scatter.3.cloned.1.call-start = ((), (), s32[]{:S(2)}) async-start(), calls=%async_computation.4 | async-start | bytes 4325376 | tf_op jit(solution)/shard_map/reduce_scatter | solution.py:183
  228.4 3.2 collective-permute-start.11
  229.8 82.5 %collective-permute-start.9 = (f32[256,128]{1,0:T(8,128)S(1)}, f32[256,128]{1,0:T(8,128)S(1)}, u32[]{:S(2)}, u32[]{:S(2)}) collective-permute-start(f32[256,128]{1,0:T(8,128)S(1)} %slice.157), channel_id=1, source_target_pairs={{4,0},{8,4},{12,8},{16,12},{20,16},{24,20},{28,24},{32,28},{36,32}... | collective-permute-start | bytes 393224 | tf_op jit(solution)/shard_map/ppermute | solution.py:19
  235.2 78.0 %collective-permute-start.8 = (bf16[256,8,128]{2,1,0:T(8,128)(2,1)S(1)}, bf16[256,8,128]{2,1,0:T(8,128)(2,1)S(1)}, u32[]{:S(2)}, u32[]{:S(2)}) collective-permute-start(bf16[256,8,128]{2,1,0:T(8,128)(2,1)S(1)} %get-tuple-element.201), channel_id=1, source_target_pairs={{0,1},{1,0},{2,3},{3,2},{4,5},{5,4},{6,7},{7,6},{8,9},{9,8},{10,11... | collective-permute-start | bytes 1572872 | tf_op jit(solution)/shard_map/ppermute | solution.py:13
  416.8 89.1 %collective-permute-start.12 = (bf16[256,128]{1,0:T(8,128)(2,1)S(1)}, bf16[256,128]{1,0:T(8,128)(2,1)S(1)}, u32[]{:S(2)}, u32[]{:S(2)}) collective-permute-start(bf16[256,128]{1,0:T(8,128)(2,1)S(1)} %get-tuple-element.205), channel_id=1, source_target_pairs={{0,1},{1,0},{2,3},{3,2},{4,5},{5,4},{6,7},{7,6},{8,9},{9,8},{10,11... | collective-permute-start | bytes 196616 | tf_op jit(solution)/shard_map/ppermute | solution.py:13
  502.2 4.3 collective-permute-start.10
Sparse Core Ops, SparseCore 0:
  18.0 98.2 all-reduce.6
  119.3 42.8 all-gather.2
  164.7 43.2 all-gather.4
  212.0 99.2 all-reduce.4
  314.9 101.0 reduce-scatter.4
  419.9 81.3 reduce-scatter.2
where the time goes:
time: 517 us; the launch traced here: 515 us
  waiting for transfers between devices  418 us (81%)
  matrix products  30.4 us (6%)
  starting transfers between devices  19.9 us (4%)
  local copies, waits for them, and re-layouts  18.5 us (4%)
  between operations  16.5 us (3%)
  other arithmetic  11.2 us (2%)
    reduce_scatter x1, waiting for transfers between devices, shards(): lax.psum_scatter(value_sum, 'ctx', scatter_dimension=0, tiled=True)  103 us
    reduce_scatter x1, waiting for transfers between devices, shards(): lax.psum_scatter(key_sum, 'ctx', scatter_dimension=0, tiled=True)  82.8 us
    psum x1, waiting for transfers between devices, shards(): lax.psum((key_part[:SINK_MAX], value_part[:SINK_MAX]), 'ctx')  74.7 us
    psum x1, waiting for transfers between devices, spread(): return lax.psum(kept, axis)  73.9 us
    all_gather x1, waiting for transfers between devices, shards(): lax.all_gather(full_values, 'ctx', axis=0, tiled=True)  45.8 us
    all_gather x1, waiting for transfers between devices, shards(): lax.all_gather(full_keys, 'ctx', axis=0, tiled=True)  30.5 us
    ppermute x9, starting transfers between devices, from_partner(): return lax.ppermute(value, axis, pairs)  10.9 us
  transfers between devices with their start and end apart: 19, of which 9 were waited for; matrix products, arithmetic and copies ran while one was open for 11% of the time, Pallas kernels for 0%

commit v1 on v0

v1 whole, which is shorter than its diff:
```python
import functools

import jax
import jax.numpy as jnp
from jax import lax
from jax.experimental import pallas as pl
from jax.experimental.pallas import tpu as pltpu
from jax.sharding import PartitionSpec as P

SINK = 128
MESH = pl.DeviceIdType.MESH
LOG2E = 1.4426950408889634
f32 = jnp.float32
bf16 = jnp.bfloat16


def dot(a, b):
    return lax.dot_general(a, b, (((1,), (0,)), ((), ())), preferred_element_type=f32)


def kernel(
    n,
    kind,
    sinks,
    windows,
    q_in,
    kv_in,
    do_in,
    aux_in,
    dq_out,
    dkv_out,
    q3,
    do3,
    kv3,
    aux3,
    kv_all,
    part,
    rpart,
    band_kv,
    halo,
    sink,
    sink_send,
    sink_recv,
    back_send,
    back_recv,
    q_t,
    do_t,
    q_r,
    do_r,
    aux_r,
    dq_t,
    dq_band,
    dq_near,
    dq_away,
    dq_home,
    dkv_own,
    dkv_band,
    dkv_near,
    dkv_away,
    dkv_home,
    local_sem,
    swap_send,
    swap_recv,
    kv_send,
    kv_recv,
    part_send,
    part_recv,
    sink_ss,
    sink_rs,
    sgrad_ss,
    sgrad_rs,
    edge_sem,
):
    tok = kv_all.shape[2]
    heads = q_in.shape[2]
    hd = q_in.shape[3]
    rows = tok * heads
    scale = hd ** (-0.5)
    me = lax.axis_index("ctx")
    g = lax.axis_index("hg")
    pg = g + 1 - 2 * lax.rem(g, 2)

    def remote(src, dst, ss, rs, ctx, hg):
        return pltpu.make_async_remote_copy(
            src_ref=src, dst_ref=dst, send_sem=ss, recv_sem=rs, device_id=(ctx, hg), device_id_type=MESH
        )

    local = []
    for slot in range(2):
        local.append((kv_in.at[slot], kv3.at[slot]))
        local.append((q_in.at[:, slot], q3.at[slot]))
        local.append((do_in.at[:, slot], do3.at[slot]))
        local.append((aux_in.at[slot], aux3.at[slot]))
    local = [pltpu.make_async_copy(a, b, local_sem.at[i]) for i, (a, b) in enumerate(local)]
    for c in local:
        c.start()

    barrier = pltpu.get_barrier_semaphore()

    def greet(s, _):
        pl.semaphore_signal(barrier, inc=1, device_id=(lax.rem(me + s, n), g), device_id_type=MESH)
        return 0

    pl.semaphore_signal(barrier, inc=1, device_id=(me, pg), device_id_type=MESH)
    lax.fori_loop(1, n, greet, 0)
    pl.semaphore_wait(barrier, n)

    swaps = [
        remote(kv_in.at[1], kv3.at[2], swap_send.at[0], swap_recv.at[0], me, pg),
        remote(aux_in.at[1], aux3.at[2], swap_send.at[1], swap_recv.at[1], me, pg),
        remote(q_in.at[:, 1], q3.at[2], swap_send.at[2], swap_recv.at[2], me, pg),
        remote(do_in.at[:, 1], do3.at[2], swap_send.at[3], swap_recv.at[3], me, pg),
    ]
    for c in swaps:
        c.start()

    first_ret = kind[2 * g] == 1
    pair = kind[2 * g] + kind[2 * g + 1] == 1
    other_slot = jnp.where(pair, 1, 2)
    full_slot = jnp.where(first_ret, 0, other_slot)
    band_slot = jnp.where(first_ret, other_slot, 0)
    other_id = jnp.where(pair, 2 * g + 1, 2 * pg + 1)
    band_id = jnp.where(first_ret, other_id, 2 * g)
    sink_count = sinks[band_id]
    window = windows[band_id]

    for c in local:
        c.wait()
    swaps[0].wait_recv()
    kv_all[me] = kv3[full_slot]
    band_kv[...] = kv3[band_slot]

    def kv_copy(block, dst):
        return remote(kv_all.at[block], kv_all.at[block], kv_send.at[dst], kv_recv.at[block], dst, g)

    def sink_copy(dst):
        return remote(band_kv.at[:, pl.ds(0, SINK)], sink, sink_ss.at[dst], sink_rs, dst, g)

    halo_copy = remote(band_kv, halo, edge_sem.at[0], edge_sem.at[1], lax.rem(me + 1, n), g)

    @pl.when(me < n - 1)
    def _():
        halo_copy.start()

    @pl.when(me == 0)
    def _():
        halo[...] = jnp.zeros_like(halo)
        sink[...] = band_kv[:, pl.ds(0, SINK)]

        def send(dst, _):
            sink_copy(dst).start()
            return 0

        lax.fori_loop(1, n, send, 0)

    def send_kv(dst, _):
        kv_copy(me, dst).start()
        return 0

    lax.fori_loop(me + 1, n, send_kv, 0)

    for c in swaps[1:]:
        c.wait_recv()

    def load_head(slot):
        q = q3[slot].reshape(rows, hd)
        d = do3[slot].reshape(rows, hd)
        q_r[...] = q
        do_r[...] = d
        q_t[...] = q.T
        do_t[...] = d.T
        aux_r[...] = aux3[slot]

    def block(k, v, allowed):
        s = dot(k, q_t[...])
        p = jnp.exp2(s * (scale * LOG2E) - aux_r[0:1, :])
        if allowed is not None:
            p = jnp.where(allowed, p, 0.0)
        dp = dot(v, do_t[...])
        ds = (p * (dp - aux_r[1:2, :])).astype(bf16)
        dv = dot(p.astype(bf16), do_r[...])
        dk = dot(ds, q_r[...])
        dq_t[...] += dot(k.T, ds)
        return dk * scale, dv

    def positions(count):
        key = lax.broadcasted_iota(jnp.int32, (count, rows), 0)
        row = lax.broadcasted_iota(jnp.int32, (count, rows), 1) // heads
        return key, row

    load_head(band_slot)
    dq_t[...] = jnp.zeros_like(dq_t)
    key, row = positions(tok)
    gap = row - key
    dk, dv = block(band_kv[0], band_kv[1], (gap >= 0) & (gap < window))
    dkv_band[0] = dk
    dkv_band[1] = dv

    @pl.when(me > 0)
    def _():
        halo_copy.wait_recv()
        sink_copy(0).wait_recv()

    dk, dv = block(halo[0], halo[1], (gap < window - tok) & (me > 0))
    back_send[0] = dk.astype(bf16)
    back_send[1] = dv.astype(bf16)
    back_copy = remote(back_send, back_recv, edge_sem.at[2], edge_sem.at[3], lax.rem(me + n - 1, n), g)

    @pl.when(me > 0)
    def _():
        back_copy.start()

    key, row = positions(SINK)
    dk, dv = block(sink[0], sink[1], (key < sink_count) & (row - key >= window - me * tok))
    sink_send[0] = dk.astype(bf16)
    sink_send[1] = dv.astype(bf16)

    def sgrad_copy(src):
        return remote(sink_send, sink_recv.at[src], sgrad_ss, sgrad_rs.at[src], 0, g)

    @pl.when(me > 0)
    def _():
        sgrad_copy(me).start()

    @pl.when(me == 0)
    def _():
        dkv_band[:, pl.ds(0, SINK)] += jnp.stack([dk, dv])

    dq_band[...] = (dq_t[...] * scale).T.astype(bf16)

    load_head(full_slot)
    dq_t[...] = jnp.zeros_like(dq_t)
    key, row = positions(tok)
    dk, dv = block(kv_all[me, 0], kv_all[me, 1], key <= row)
    dkv_own[0] = dk
    dkv_own[1] = dv

    def part_copy(blk, src):
        return remote(part.at[blk], rpart.at[src], part_send.at[blk], part_recv.at[src], blk, g)

    def step(s, _):
        j = me - s
        kv_copy(j, me).wait_recv()
        dk, dv = block(kv_all[j, 0], kv_all[j, 1], None)
        part[j, 0] = dk.astype(bf16)
        part[j, 1] = dv.astype(bf16)
        part_copy(j, me).start()
        return 0

    lax.fori_loop(1, me + 1, step, 0)

    dq_full = (dq_t[...] * scale).T.astype(bf16)
    band = dq_band[...]
    dq_near[...] = jnp.where(first_ret, dq_full, band).reshape(tok, heads, hd)
    dq_away[...] = jnp.where(first_ret, band, dq_full).reshape(tok, heads, hd)
    back_q = remote(dq_away, dq_home, swap_send.at[4], swap_recv.at[4], me, pg)
    back_q.start()
    out_near = pltpu.make_async_copy(dq_near, dq_out.at[:, 0], local_sem.at[0])
    out_near.start()

    @pl.when(me < n - 1)
    def _():
        back_copy.wait_recv()
        dkv_band[...] += back_recv[...].astype(f32)

    @pl.when(me == 0)
    def _():
        def add(src, _):
            sgrad_copy(src).wait_recv()
            dkv_band[:, pl.ds(0, SINK)] += sink_recv[src].astype(f32)
            return 0

        lax.fori_loop(1, n, add, 0)

    def add(src, _):
        part_copy(me, src).wait_recv()
        dkv_own[...] += rpart[src].astype(f32)
        return 0

    lax.fori_loop(me + 1, n, add, 0)

    full = dkv_own[...].astype(bf16)
    band = dkv_band[...].astype(bf16)
    dkv_near[...] = jnp.where(first_ret, full, band)
    dkv_away[...] = jnp.where(first_ret, band, full)
    back_kv = remote(dkv_away, dkv_home, swap_send.at[5], swap_recv.at[5], me, pg)
    back_kv.start()
    dkv_out[0] = dkv_near[...]

    back_q.wait()
    dq_home[...] = jnp.where(pair, dq_away[...], dq_home[...])
    out_far = pltpu.make_async_copy(dq_home, dq_out.at[:, 1], local_sem.at[1])
    out_far.start()
    back_kv.wait()
    dkv_out[1] = jnp.where(pair, dkv_away[...], dkv_home[...])

    for c in swaps:
        c.wait_send()

    def drain_kv(dst, _):
        kv_copy(me, dst).wait_send()
        return 0

    lax.fori_loop(me + 1, n, drain_kv, 0)

    def drain_part(blk, _):
        part_copy(blk, me).wait_send()
        return 0

    lax.fori_loop(0, me, drain_part, 0)

    @pl.when(me < n - 1)
    def _():
        halo_copy.wait_send()

    @pl.when(me > 0)
    def _():
        back_copy.wait_send()
        sgrad_copy(me).wait_send()

    @pl.when(me == 0)
    def _():
        def drain(dst, _):
            sink_copy(dst).wait_send()
            return 0

        lax.fori_loop(1, n, drain, 0)

    out_near.wait()
    out_far.wait()


def shards(queries, keys, values, outputs, grads, logs, kind, sinks, windows):
    tok, _, heads, hd = queries.shape
    rows = tok * heads
    n = lax.axis_size("ctx")
    delta = jnp.sum(grads.astype(f32) * outputs.astype(f32), axis=-1)
    lse = logs.astype(f32) * LOG2E
    aux = jnp.stack([lse, delta], axis=0)
    aux = jnp.moveaxis(aux, 2, 0).reshape(2, 2, rows)
    aux = jnp.pad(aux, ((0, 0), (0, 6), (0, 0)))
    kv = jnp.moveaxis(jnp.stack([keys, values], axis=0), 2, 0)
    smem = pl.BlockSpec(memory_space=pltpu.SMEM)
    hbm = pl.BlockSpec(memory_space=pl.ANY)
    vmem = pl.BlockSpec(memory_space=pltpu.VMEM)
    V = pltpu.VMEM
    dma = pltpu.SemaphoreType.DMA
    dq, dkv = pl.pallas_call(
        functools.partial(kernel, n),
        in_specs=[smem, smem, smem, hbm, hbm, hbm, hbm],
        out_specs=[hbm, vmem],
        out_shape=[
            jax.ShapeDtypeStruct((tok, 2, heads, hd), bf16),
            jax.ShapeDtypeStruct((2, 2, tok, hd), bf16),
        ],
        scratch_shapes=[
            V((3, tok, heads, hd), bf16),
            V((3, tok, heads, hd), bf16),
            V((3, 2, tok, hd), bf16),
            V((3, 8, rows), f32),
            V((n, 2, tok, hd), bf16),
            V((n, 2, tok, hd), bf16),
            V((n, 2, tok, hd), bf16),
            V((2, tok, hd), bf16),
            V((2, tok, hd), bf16),
            V((2, SINK, hd), bf16),
            V((2, SINK, hd), bf16),
            V((n, 2, SINK, hd), bf16),
            V((2, tok, hd), bf16),
            V((2, tok, hd), bf16),
            V((hd, rows), bf16),
            V((hd, rows), bf16),
            V((rows, hd), bf16),
            V((rows, hd), bf16),
            V((8, rows), f32),
            V((hd, rows), f32),
            V((rows, hd), bf16),
            V((tok, heads, hd), bf16),
            V((tok, heads, hd), bf16),
            V((tok, heads, hd), bf16),
            V((2, tok, hd), f32),
            V((2, tok, hd), f32),
            V((2, tok, hd), bf16),
            V((2, tok, hd), bf16),
            V((2, tok, hd), bf16),
            dma((8,)),
            dma((6,)),
            dma((6,)),
            dma((n,)),
            dma((n,)),
            dma((n,)),
            dma((n,)),
            dma((n,)),
            dma,
            dma,
            dma((n,)),
            dma((4,)),
        ],
        compiler_params=pltpu.CompilerParams(
            collective_id=0, has_side_effects=True, vmem_limit_bytes=60 * 2**20
        ),
        name="attention_grads",
    )(kind, sinks, windows, queries, kv, grads, aux)
    dkv = jnp.moveaxis(dkv, 0, 2)
    return dq, dkv[0], dkv[1]


def solution(mesh):
    return jax.shard_map(
        shards,
        mesh=mesh,
        in_specs=(
            P("ctx", "hg", None, None),
            P("ctx", "hg", None),
            P("ctx", "hg", None),
            P("ctx", "hg", None, None),
            P("ctx", "hg", None, None),
            P("ctx", "hg", None),
            P(),
            P(),
            P(),
        ),
        out_specs=(P("ctx", "hg", None, None), P("ctx", "hg", None), P("ctx", "hg", None)),
        check_vma=False,
    )
```

time: 517 us -> 136 us (0.26)
  waiting for transfers between devices: 418 us -> 0 us
  Pallas kernels: 0 us -> 127 us
  matrix products: 30.4 us -> 0 us
  starting transfers between devices: 19.9 us -> 0 us
  between operations: 16.5 us -> 0.69 us
  local copies, waits for them, and re-layouts: 18.5 us -> 4.94 us
  other arithmetic: 11.2 us -> 3.8 us
    reduce_scatter x2 -> x0, waiting for transfers between devices: 186 us -> none  [the longest x1 103 us: shards(): lax.psum_scatter(value_sum, 'ctx', scatter_dimension=0, tiled=True)]
    psum x2 -> x0, waiting for transfers between devices: 149 us -> none  [the longest x1 74.7 us: shards(): lax.psum((key_part[:SINK_MAX], value_part[:SINK_MAX]), 'ctx')]
    pallas_call x0 -> x1, Pallas kernels: none -> 127 us  [shards(): pl.pallas_call(functools.partial(kernel, n), in_specs=[smem, smem, smem,...]
    all_gather x2 -> x0, waiting for transfers between devices: 76.3 us -> none  [the longest x1 45.8 us: shards(): lax.all_gather(full_values, 'ctx', axis=0, tiled=True)]
    dot_general x10 -> x0, matrix products: 30.4 us -> none  [the longest x2 8.61 us: block_grads(): jnp.einsum('qd,kd->qk', query_vecs, key_block, preferred_element_type=jnp...]
    ppermute x13 -> x0, starting transfers between devices: 19.6 us -> none  [the longest x9 10.9 us: from_partner(): return lax.ppermute(value, axis, pairs)]
    ppermute x13 -> x0, waiting for transfers between devices: 6.77 us -> none  [the longest x9 6.14 us: from_partner(): return lax.ppermute(value, axis, pairs)]
  transfers between devices with their start and end apart: 19 -> 0, of which waited for: 9 -> 0; matrix products, arithmetic and copies ran while one was open for 11% -> 0% of each run, Pallas kernels for 0% -> 0%
where the time goes in v1:
time: 136 us
  Pallas kernels  127 us (93%)
  local copies, waits for them, and re-layouts  4.94 us (4%)
  other arithmetic  3.8 us (3%)
    pallas_call x1, Pallas kernels, shards(): pl.pallas_call(functools.partial(kernel, n), in_specs=[smem, smem, smem,...  127 us

profile of v1, /device:TPU:0, one launch (start us, length us, event | category | flops | bytes accessed | tf_op | source)
XLA Modules:
  0.0 136.2 jit_solution(15611196637450405372)
XLA Ops:
  0.6 0.7 multiply_bitcast_fusion
  1.3 0.0 copy-start.1
  1.3 0.0 copy-start.2
  1.3 2.4 %multiply_reduce_fusion = f32[256,2,8]{2,1,0:T(2,128)S(1)} fusion(bf16[256,2,8,128]{3,2,1,0:T(8,128)(2,1)} %param.12, bf16[256,2,8,128]{3,2,1,0:T(8,128)(2,1)} %do_in.1), kind=kLoop, calls=%fused_computation | loop fusion | flops 2093056 | bytes 2113536 | tf_op jit(solution)/shard_map/reduce_sum | solution.py:337
  3.7 0.1 copy.30
  3.8 0.0 copy-done.1
  3.8 0.0 copy-done.2
  3.9 0.7 maximum_bitcast_fusion.kv_in
  4.6 0.2 copy.31
  4.8 0.3 reshape.9
  5.1 0.7 pad.4.aux_in
  5.8 126.7 %attention_grads.1 = (bf16[256,2,8,128]{3,2,1,0:T(8,128)(2,1)}, bf16[2,2,256,128]{3,2,1,0:T(8,128)(2,1)}) custom-call(s32[8]{0:T(128)} %kind.1, s32[8]{0:T(128)} %sinks.1, s32[8]{0:T(128)} %windows.1, bf16[256,2,8,128]{3,2,1,0:T(8,128)(2,1)} %q_in.1, bf16[2,2,256,128]{3,2,1,0:T(8,128)(2,1)} %maximum_bitcast_fusion.kv_in, bf16[256,2,8,128]{3,2,1,0:T(8,128)(2,1)} %do_in.1, ...), custom_call_target="tpu_custom_call" | custom-call | tf_op jit(solution)/shard_map/attention_grads/pallas_call | solution.py:348
  132.5 0.0 copy-start
  132.5 1.1 slice_bitcast_fusion
  133.6 0.8 copy.33
  134.4 0.8 copy.32
  135.2 0.0 copy-done
  135.2 1.0 copy.37
  (2 shorter events, 0.0 us)
Async XLA Ops:
  1.3 2.5 %copy-start.1 = (bf16[256,2,128]{2,1,0:T(2,128)(2,1)S(1)}, bf16[256,2,128]{2,1,0:T(2,128)(2,1)}, u32[]{:S(2)}) copy-start(bf16[256,2,128]{2,1,0:T(2,128)(2,1)} %param.11) | copy-start | bytes 393220
  1.3 2.5 %copy-start.2 = (bf16[256,2,128]{2,1,0:T(2,128)(2,1)S(1)}, bf16[256,2,128]{2,1,0:T(2,128)(2,1)}, u32[]{:S(2)}) copy-start(bf16[256,2,128]{2,1,0:T(2,128)(2,1)} %param.10) | copy-start | bytes 393220
  132.5 2.7 %copy-start = (bf16[256,2,8,128]{3,2,1,0:T(8,128)(2,1)S(1)}, bf16[256,2,8,128]{3,2,1,0:T(8,128)(2,1)}, u32[]{:S(2)}) copy-start(bf16[256,2,8,128]{3,2,1,0:T(8,128)(2,1)} %get-tuple-element.26) | copy-start | bytes 3145732

commit v2 on v1

--- a/solution.py
+++ b/solution.py
@@ -8,6 +8,7 @@
 from jax.sharding import PartitionSpec as P
 
 SINK = 128
+AHEAD = 4
 MESH = pl.DeviceIdType.MESH
 LOG2E = 1.4426950408889634
 f32 = jnp.float32
@@ -36,6 +37,8 @@
     kv_all,
     part,
     rpart,
+    spart,
+    pown,
     band_kv,
     halo,
     sink,
@@ -63,8 +66,10 @@
     swap_recv,
     kv_send,
     kv_recv,
+    fwd_send,
     part_send,
     part_recv,
+    spart_recv,
     sink_ss,
     sink_rs,
     sgrad_ss,
@@ -79,6 +84,10 @@
     me = lax.axis_index("ctx")
     g = lax.axis_index("hg")
     pg = g + 1 - 2 * lax.rem(g, 2)
+    chips = n // 2
+    chip = me // 2
+    core = lax.rem(me, 2)
+    sib = me + 1 - 2 * core
 
     def remote(src, dst, ss, rs, ctx, hg):
         return pltpu.make_async_remote_copy(
@@ -153,11 +162,27 @@
 
         lax.fori_loop(1, n, send, 0)
 
-    def send_kv(dst, _):
-        kv_copy(me, dst).start()
-        return 0
-
-    lax.fori_loop(me + 1, n, send_kv, 0)
+    @pl.when(core == 0)
+    def _():
+        kv_copy(me, sib).start()
+
+    def send_kv(at, _):
+        kv_copy(me, 2 * at + core).start()
+        return 0
+
+    lax.fori_loop(chip + 1, chips, send_kv, 0)
+
+    def forward_copy(at):
+        blk = 2 * at + core
+        return remote(kv_all.at[blk], kv_all.at[blk], fwd_send.at[at], kv_recv.at[blk], sib, g)
+
+    def forward(i, _):
+        at = chip - 1 - i
+        kv_copy(2 * at + core, me).wait_recv()
+        forward_copy(at).start()
+        return 0
+
+    lax.fori_loop(0, jnp.minimum(AHEAD, chip), forward, 0)
 
     for c in swaps[1:]:
         c.wait_recv()
@@ -238,16 +263,53 @@
     def part_copy(blk, src):
         return remote(part.at[blk], rpart.at[src], part_send.at[blk], part_recv.at[src], blk, g)
 
-    def step(s, _):
-        j = me - s
-        kv_copy(j, me).wait_recv()
-        dk, dv = block(kv_all[j, 0], kv_all[j, 1], None)
-        part[j, 0] = dk.astype(bf16)
-        part[j, 1] = dv.astype(bf16)
-        part_copy(j, me).start()
-        return 0
-
-    lax.fori_loop(1, me + 1, step, 0)
+    def spart_copy(at):
+        blk = 2 * at + 1 - core
+        return remote(part.at[blk], spart.at[at], part_send.at[blk], spart_recv.at[at], sib, g)
+
+    @pl.when(core == 1)
+    def _():
+        kv_copy(sib, me).wait_recv()
+        dk, dv = block(kv_all[sib, 0], kv_all[sib, 1], None)
+        part[sib, 0] = dk.astype(bf16)
+        part[sib, 1] = dv.astype(bf16)
+        part_copy(sib, me).start()
+
+    def combine(at):
+        blk = 2 * at + core
+        spart_copy(at).wait_recv()
+        part[blk] = (pown[at] + spart[at].astype(f32)).astype(bf16)
+        part_copy(blk, me).start()
+
+    def step(t, _):
+        at = chip - t
+        mine = 2 * at + core
+        theirs = 2 * at + 1 - core
+
+        @pl.when(t - 1 + AHEAD < chip)
+        def _():
+            forward(t - 1 + AHEAD, 0)
+
+        kv_copy(theirs, me).wait_recv()
+        dk, dv = block(kv_all[theirs, 0], kv_all[theirs, 1], None)
+        part[theirs, 0] = dk.astype(bf16)
+        part[theirs, 1] = dv.astype(bf16)
+        spart_copy(at).start()
+        dk, dv = block(kv_all[mine, 0], kv_all[mine, 1], None)
+        pown[at, 0] = dk
+        pown[at, 1] = dv
+
+        @pl.when(t > 1)
+        def _():
+            combine(at + 1)
+
+        return 0
+
+    lax.fori_loop(1, chip + 1, step, 0)
+
+    @pl.when(chip > 0)
+    def _():
+        combine(0)
 
     dq_full = (dq_t[...] * scale).T.astype(bf16)
     band = dq_band[...]
@@ -272,12 +334,19 @@
 
         lax.fori_loop(1, n, add, 0)
 
-    def add(src, _):
+    def take(src):
         part_copy(me, src).wait_recv()
         dkv_own[...] += rpart[src].astype(f32)
-        return 0
-
-    lax.fori_loop(me + 1, n, add, 0)
+
+    @pl.when(core == 0)
+    def _():
+        take(sib)
+
+    def add(at, _):
+        take(2 * at + core)
+        return 0
+
+    lax.fori_loop(chip + 1, chips, add, 0)
 
     full = dkv_own[...].astype(bf16)
     band = dkv_band[...].astype(bf16)
@@ -297,11 +366,21 @@
     for c in swaps:
         c.wait_send()
 
-    def drain_kv(dst, _):
-        kv_copy(me, dst).wait_send()
-        return 0
-
-    lax.fori_loop(me + 1, n, drain_kv, 0)
+    @pl.when(core == 0)
+    def _():
+        kv_copy(me, sib).wait_send()
+
+    def drain_kv(at, _):
+        kv_copy(me, 2 * at + core).wait_send()
+        return 0
+
+    lax.fori_loop(chip + 1, chips, drain_kv, 0)
+
+    def drain_forward(at, _):
+        forward_copy(at).wait_send()
+        return 0
+
+    lax.fori_loop(0, chip, drain_forward, 0)
 
     def drain_part(blk, _):
         part_copy(blk, me).wait_send()
@@ -338,7 +417,6 @@
     lse = logs.astype(f32) * LOG2E
     aux = jnp.stack([lse, delta], axis=0)
     aux = jnp.moveaxis(aux, 2, 0).reshape(2, 2, rows)
-    aux = jnp.pad(aux, ((0, 0), (0, 6), (0, 0)))
     kv = jnp.moveaxis(jnp.stack([keys, values], axis=0), 2, 0)
     smem = pl.BlockSpec(memory_space=pltpu.SMEM)
     hbm = pl.BlockSpec(memory_space=pl.ANY)
@@ -357,10 +435,12 @@
             V((3, tok, heads, hd), bf16),
             V((3, tok, heads, hd), bf16),
             V((3, 2, tok, hd), bf16),
-            V((3, 8, rows), f32),
+            V((3, 2, rows), f32),
             V((n, 2, tok, hd), bf16),
             V((n, 2, tok, hd), bf16),
             V((n, 2, tok, hd), bf16),
+            V((n // 2, 2, tok, hd), bf16),
+            V((n // 2, 2, tok, hd), f32),
             V((2, tok, hd), bf16),
             V((2, tok, hd), bf16),
             V((2, SINK, hd), bf16),
@@ -372,7 +452,7 @@
             V((hd, rows), bf16),
             V((rows, hd), bf16),
             V((rows, hd), bf16),
-            V((8, rows), f32),
+            V((2, rows), f32),
             V((hd, rows), f32),
             V((rows, hd), bf16),
             V((tok, heads, hd), bf16),
@@ -388,8 +468,10 @@
             dma((6,)),
             dma((n,)),
             dma((n,)),
+            dma((n // 2,)),
             dma((n,)),
             dma((n,)),
+            dma((n // 2,)),
             dma((n,)),
             dma,
             dma,

time: 136 us -> 119 us (0.88); the launches traced: 136 us -> 117 us
  Pallas kernels: 127 us -> 108 us
    pallas_call x1, Pallas kernels: 127 us -> 108 us  [shards(): pl.pallas_call(functools.partial(kernel, n), in_specs=[smem, smem, smem,...]
where the time goes in v2:
time: 119 us; the launch traced here: 117 us
  Pallas kernels  108 us (91%)
  local copies, waits for them, and re-layouts  4.88 us (4%)
  other arithmetic  3.8 us (3%)
    pallas_call x1, Pallas kernels, shards(): pl.pallas_call(functools.partial(kernel, n), in_specs=[smem, smem, smem,...  108 us
    unnamed x9, local copies, waits for them, and re-layouts  2.57 us

profile of v2, /device:TPU:0, one launch (start us, length us, event | category | flops | bytes accessed | tf_op | source)
XLA Modules:
  0.0 117.3 jit_solution(14507915665644202340)
XLA Ops:
  0.6 0.7 multiply_bitcast_fusion
  1.3 0.0 copy-start.1
  1.3 0.0 copy-start.2
  1.3 2.4 %multiply_reduce_fusion = f32[256,2,8]{2,1,0:T(2,128)S(1)} fusion(bf16[256,2,8,128]{3,2,1,0:T(8,128)(2,1)} %param.12, bf16[256,2,8,128]{3,2,1,0:T(8,128)(2,1)} %do_in.1), kind=kLoop, calls=%fused_computation | loop fusion | flops 2093056 | bytes 2113536 | tf_op jit(solution)/shard_map/reduce_sum | solution.py:416
  3.7 0.1 copy.30
  3.8 0.0 copy-done.1
  3.8 0.0 copy-done.2
  3.9 0.7 maximum_bitcast_fusion.kv_in
  4.6 0.2 copy.31
  4.8 0.9 reshape.9.aux_in
  5.7 107.9 %attention_grads.1 = (bf16[256,2,8,128]{3,2,1,0:T(8,128)(2,1)}, bf16[2,2,256,128]{3,2,1,0:T(8,128)(2,1)}) custom-call(s32[8]{0:T(128)} %kind.1, s32[8]{0:T(128)} %sinks.1, s32[8]{0:T(128)} %windows.1, bf16[256,2,8,128]{3,2,1,0:T(8,128)(2,1)} %q_in.1, bf16[2,2,256,128]{3,2,1,0:T(8,128)(2,1)} %maximum_bitcast_fusion.kv_in, bf16[256,2,8,128]{3,2,1,0:T(8,128)(2,1)} %do_in.1, ...), custom_call_target="tpu_custom_call" | custom-call | tf_op jit(solution)/shard_map/attention_grads/pallas_call | solution.py:426
  113.6 0.0 copy-start
  113.6 1.1 slice_bitcast_fusion
  114.7 0.8 copy.33
  115.5 0.8 copy.32
  116.3 0.0 copy-done
  116.3 1.0 copy.37
  (2 shorter events, 0.0 us)
Async XLA Ops:
  1.3 2.5 %copy-start.1 = (bf16[256,2,128]{2,1,0:T(2,128)(2,1)S(1)}, bf16[256,2,128]{2,1,0:T(2,128)(2,1)}, u32[]{:S(2)}) copy-start(bf16[256,2,128]{2,1,0:T(2,128)(2,1)} %param.11) | copy-start | bytes 393220
  1.3 2.5 %copy-start.2 = (bf16[256,2,128]{2,1,0:T(2,128)(2,1)S(1)}, bf16[256,2,128]{2,1,0:T(2,128)(2,1)}, u32[]{:S(2)}) copy-start(bf16[256,2,128]{2,1,0:T(2,128)(2,1)} %param.10) | copy-start | bytes 393220
  113.6 2.7 %copy-start = (bf16[256,2,8,128]{3,2,1,0:T(8,128)(2,1)S(1)}, bf16[256,2,8,128]{3,2,1,0:T(8,128)(2,1)}, u32[]{:S(2)}) copy-start(bf16[256,2,8,128]{3,2,1,0:T(8,128)(2,1)} %get-tuple-element.26) | copy-start | bytes 3145732

commit v3 on v1

v3 whole, which is shorter than its diff:
```python
import functools

import jax
import jax.numpy as jnp
from jax import lax
from jax.experimental import pallas as pl
from jax.experimental.pallas import tpu as pltpu
from jax.sharding import PartitionSpec as P

SINK = 128
MESH = pl.DeviceIdType.MESH
LOG2E = 1.4426950408889634
f32 = jnp.float32
bf16 = jnp.bfloat16


def dot(a, b):
    return lax.dot_general(a, b, (((1,), (0,)), ((), ())), preferred_element_type=f32)


def kernel(
    n,
    kind,
    sinks,
    windows,
    q_in,
    kv_in,
    do_in,
    aux_in,
    dq_out,
    dkv_out,
    q3,
    do3,
    kv3,
    aux3,
    kv_all,
    pown,
    part,
    x_part,
    hop_part,
    z_part,
    sib_part,
    spart,
    halo,
    sink,
    sink_sum,
    sink_send,
    sink_recv,
    back_send,
    back_recv,
    q_t,
    do_t,
    q_r,
    do_r,
    dq_t,
    dq_band,
    dq_full,
    dq_near,
    dq_home,
    dkv_own,
    dkv_band,
    dkv_full,
    dkv_home,
    local_sem,
    swap_send,
    swap_recv,
    kv_recv,
    z_send,
    x_send,
    relay_send,
    fwd_send,
    part_send,
    x_recv,
    hop_recv,
    z_recv,
    sib_recv,
    spart_recv,
    sink_zs,
    sink_xs,
    sink_fs,
    sink_rs,
    sgrad_ss,
    sgrad_rs,
    edge_sem,
):
    tok = kv_all.shape[2]
    heads = q_in.shape[2]
    hd = q_in.shape[3]
    rows = tok * heads
    scale = hd ** (-0.5)
    me = lax.axis_index("ctx")
    g = lax.axis_index("hg")
    pg = g + 1 - 2 * lax.rem(g, 2)
    chips = n // 2
    chip = me // 2
    core = lax.rem(me, 2)
    nx = min(4, chips)
    nz = chips // nx
    z = chip // nx
    x = lax.rem(chip, nx)
    turn = 1 - 2 * core
    sib = me + turn
    beside = lax.rem(me - turn + n, n)
    after = lax.rem(me + 1, n)
    before = lax.rem(me + n - 1, n)

    def remote(src, dst, ss, rs, ctx, hg):
        return pltpu.make_async_remote_copy(
            src_ref=src, dst_ref=dst, send_sem=ss, recv_sem=rs, device_id=(ctx, hg), device_id_type=MESH
        )

    def at_place(pz, px, pc):
        return (pz * nx + px) * 2 + pc

    def loop(lo, hi, body):
        def one(i, _):
            body(i)
            return 0

        lax.fori_loop(lo, hi, one, 0)

    local = []
    for slot in range(2):
        local.append((kv_in.at[slot], kv3.at[slot]))
        local.append((q_in.at[:, slot], q3.at[slot]))
        local.append((do_in.at[:, slot], do3.at[slot]))
        local.append((aux_in.at[slot], aux3.at[slot]))
    local = [pltpu.make_async_copy(a, b, local_sem.at[i]) for i, (a, b) in enumerate(local)]
    for c in local:
        c.start()

    barrier = pltpu.get_barrier_semaphore()

    def greet(ctx, hg):
        pl.semaphore_signal(barrier, inc=1, device_id=(ctx, hg), device_id_type=MESH)

    greet(me, pg)
    greet(sib, g)
    greet(beside, g)
    for d in range(1, nz):
        greet(at_place(lax.rem(z + d, nz), x, core), g)
    for d in range(1, nx):
        greet(at_place(z, lax.rem(x + d, nx), core), g)
    pl.semaphore_wait(barrier, 1 + nz + nx)

    pieces = [
        (kv_in.at[1], kv3.at[2]),
        (aux_in.at[1], aux3.at[2]),
        (q_in.at[:, 1], q3.at[2]),
        (do_in.at[:, 1], do3.at[2]),
    ]
    swaps = [remote(a, b, swap_send.at[i], swap_recv.at[i], me, pg) for i, (a, b) in enumerate(pieces)]
    for c in swaps:
        c.start()

    kinds = [kind[2 * g], kind[2 * g + 1]]
    first_ret = kinds[0] == 1
    second_ret = kinds[1] == 1
    pair = kinds[0] + kinds[1] == 1
    full_slot = jnp.where(first_ret, 0, jnp.where(pair, 1, 2))

    halo_copy = remote(kv_in.at[pl.ds(0, 2)], halo, edge_sem.at[0], edge_sem.at[1], after, g)

    @pl.when(me < n - 1)
    def _():
        halo_copy.start()

    def sink_copy(dst, sem):
        return remote(sink, sink, sem, sink_rs, dst, g)

    def sink_z(zd):
        return sink_copy(at_place(zd, 0, 0), sink_zs.at[zd])

    def sink_x(xd):
        return sink_copy(at_place(z, xd, 0), sink_xs.at[xd])

    for c in local:
        c.wait()

    @pl.when(me == 0)
    def _():
        halo[...] = jnp.zeros_like(halo)
        sink[...] = kv3[0:2, :, 0:SINK]
        loop(1, nz, lambda zd: sink_z(zd).start())

    def kv_copy(block, dst, sem):
        return remote(kv_all.at[block], kv_all.at[block], sem, kv_recv.at[block], dst, g)

    def kv_wait(block):
        kv_copy(block, sib, fwd_send.at[0]).wait_recv()

    def to_z(zd):
        return kv_copy(me, at_place(zd, x, core), z_send.at[zd])

    def to_x(zs, xd):
        return kv_copy(at_place(zs, x, core), at_place(z, xd, core), x_send.at[zs, xd])

    def to_sib(at):
        return kv_copy(2 * at + core, sib, fwd_send.at[at])

    def relay(zs):
        blk = at_place(zs, lax.rem(x - turn + nx, nx), core)
        return kv_copy(blk, at_place(z, lax.rem(x + turn + nx, nx), core), relay_send.at[zs])

    def load_head(slot):
        q = q3[slot].reshape(rows, hd)
        d = do3[slot].reshape(rows, hd)
        q_r[slot] = q
        do_r[slot] = d
        q_t[slot] = q.T
        do_t[slot] = d.T
        dq_t[slot] = jnp.zeros((hd, rows), f32)

    def block(slot, acc, k, v, allowed):
        s = dot(k, q_t[slot])
        p = jnp.exp2(s * (scale * LOG2E) - aux3[slot, 0:1, :])
        if allowed is not None:
            p = jnp.where(allowed, p, 0.0)
        dp = dot(v, do_t[slot])
        ds = (p * (dp - aux3[slot, 1:2, :])).astype(bf16)
        dv = dot(p.astype(bf16), do_r[slot])
        dk = dot(ds, q_r[slot])
        dq_t[acc] += dot(k.T, ds)
        return dk * scale, dv

    def query_grads(acc):
        return (dq_t[acc] * scale).T.astype(bf16).reshape(tok, heads, hd)

    def gap(count, key_start):
        key = lax.broadcasted_iota(jnp.int32, (count, rows), 0) + key_start
        row = lax.broadcasted_iota(jnp.int32, (count, rows), 1) // heads
        return row - key

    def band(slot):
        window = windows[2 * g + slot]
        dist = gap(tok, 0)
        dk, dv = block(slot, slot, kv3[slot, 0], kv3[slot, 1], (dist >= 0) & (dist < window))
        dkv_band[slot, 0] = dk
        dkv_band[slot, 1] = dv
        if slot == 0:

            @pl.when(me > 0)
            def _():
                halo_copy.wait_recv()

        dk, dv = block(slot, slot, halo[slot, 0], halo[slot, 1], (dist < window - tok) & (me > 0))
        back_send[slot, 0] = dk.astype(bf16)
        back_send[slot, 1] = dv.astype(bf16)

    def band_sink(slot):
        sink_count = sinks[2 * g + slot]
        window = windows[2 * g + slot]
        key = lax.broadcasted_iota(jnp.int32, (SINK, rows), 0)
        dist = gap(SINK, 0)
        allowed = (key < sink_count) & (dist >= window - me * tok)
        dk, dv = block(slot, slot, sink[slot, 0], sink[slot, 1], allowed)
        sink_sum[slot, 0] = dk
        sink_sum[slot, 1] = dv
        dq_band[slot] = query_grads(slot)

    load_head(0)
    load_head(1)
    swaps[0].wait_recv()
    kv_all[me] = kv3[full_slot]
    loop(z + 1, nz, lambda zd: to_z(zd).start())
    loop(x + 1, nx, lambda xd: to_x(z, xd).start())

    @pl.when(core == 0)
    def _():
        to_sib(chip).start()

    def arrive_z(i):
        zs = z - i
        kv_wait(at_place(zs, x, core))
        if nx == 4:
            to_x(zs, lax.rem(x + 1, nx)).start()
            to_x(zs, lax.rem(x + nx - 1, nx)).start()
        else:
            for d in range(1, nx):
                to_x(zs, lax.rem(x + d, nx)).start()
        to_sib(zs * nx + x).start()

    def arrive(zs, xs):
        kv_wait(at_place(zs, xs, core))
        to_sib(zs * nx + xs).start()

    def near(zs):
        if nx == 4:
            arrive(zs, lax.rem(x - turn + nx, nx))
            relay(zs).start()
            arrive(zs, lax.rem(x + turn + nx, nx))
        else:
            for d in range(1, nx):
                arrive(zs, lax.rem(x + d, nx))

    def far(zs):
        if nx == 4:
            arrive(zs, lax.rem(x + 2, nx))

    loop(1, z + 1, arrive_z)

    @pl.when((x == 0) & (core == 0))
    def _():
        @pl.when(z > 0)
        def _():
            sink_copy(sib, sink_fs).wait_recv()

        loop(1, nx, lambda xd: sink_x(xd).start())

    band(0)
    loop(0, x, lambda xs: arrive(z, xs))
    loop(1, z + 1, lambda i: near(z - i))

    @pl.when((x > 0) & (core == 0))
    def _():
        sink_copy(sib, sink_fs).wait_recv()

    @pl.when(core == 0)
    def _():
        sink_copy(sib, sink_fs).start()

    band(1)
    loop(1, z + 1, lambda i: far(z - i))

    @pl.when(core == 1)
    def _():
        sink_copy(sib, sink_fs).wait_recv()

    band_sink(0)
    band_sink(1)

    back_copy = remote(back_send, back_recv, edge_sem.at[2], edge_sem.at[3], before, g)

    @pl.when(me > 0)
    def _():
        back_copy.start()

    def sgrad_copy(slot, dst):
        return remote(sink_send, sink_recv.at[slot], sgrad_ss, sgrad_rs.at[slot], dst, g)

    def sgrad_add(slot):
        sgrad_copy(slot, sib).wait_recv()
        sink_sum[...] += sink_recv[slot].astype(f32)

    def sgrad_send(slot, dst):
        sink_send[...] = sink_sum[...].astype(bf16)
        sgrad_copy(slot, dst).start()

    @pl.when(core == 1)
    def _():
        sgrad_send(0, sib)

    def sib_copy(dst):
        return remote(part.at[dst], sib_part, part_send.at[dst], sib_recv, sib, g)

    def spart_copy(at):
        blk = 2 * at + 1 - core
        return remote(part.at[blk], spart.at[at], part_send.at[blk], spart_recv.at[at], sib, g)

    def x_copy(zs, xs, xd):
        blk = at_place(zs, xd, core)
        return remote(
            part.at[blk], x_part.at[zs, xs], part_send.at[blk], x_recv.at[zs, xs], at_place(z, xd, core), g
        )

    def z_copy(zs, zd):
        blk = at_place(zd, x, core)
        return remote(
            part.at[blk], z_part.at[zs], part_send.at[blk], z_recv.at[zs], at_place(zd, x, core), g
        )

    def hop_copy(zs):
        blk = at_place(zs, lax.rem(x + 2, nx), core)
        to = at_place(z, lax.rem(x + turn + nx, nx), core)
        return remote(part.at[blk], hop_part.at[zs], part_send.at[blk], hop_recv.at[zs], to, g)

    def combine(at):
        zs = at // nx
        xd = lax.rem(at, nx)
        spart_copy(at).wait_recv()
        blk = 2 * at + core
        pown[at] += spart[at].astype(f32)
        straight = (zs == z) | (xd != x)
        if nx == 4:
            apart = lax.rem((xd - x) * turn + nx, nx)
            straight = (zs == z) | (apart == nx - 1)

            @pl.when((zs < z) & (apart == 2))
            def _():
                part[blk] = pown[at].astype(bf16)
                hop_copy(zs).start()

        @pl.when(straight)
        def _():
            part[blk] = pown[at].astype(bf16)
            x_copy(zs, x, xd).start()

    def hop(zs):
        if nx == 4:
            xd = lax.rem(x + turn + nx, nx)
            at = zs * nx + xd
            blk = 2 * at + core
            hop_copy(zs).wait_recv()
            part[blk] = (pown[at] + hop_part[zs].astype(f32)).astype(bf16)
            x_copy(zs, x, xd).start()

    def gather_x(zs):
        at = zs * nx + x
        blk = 2 * at + core
        for d in range(1, nx):
            if nx == 4 and d == 2:
                continue
            xs = lax.rem(x + d, nx)
            x_copy(zs, xs, x).wait_recv()
            pown[at] += x_part[zs, xs].astype(f32)
        part[blk] = pown[at].astype(bf16)
        z_copy(z, zs).start()

    for c in swaps[1:]:
        c.wait_recv()
    load_head(2)
    dk, dv = block(full_slot, 2, kv_all[me, 0], kv_all[me, 1], gap(tok, 0) >= 0)
    dkv_own[0] = dk
    dkv_own[1] = dv

    @pl.when(core == 1)
    def _():
        kv_wait(sib)
        dk, dv = block(full_slot, 2, kv_all[sib, 0], kv_all[sib, 1], None)
        part[sib, 0] = dk.astype(bf16)
        part[sib, 1] = dv.astype(bf16)
        sib_copy(sib).start()

    def step(t):
        at = chip - t
        mine = 2 * at + core
        theirs = 2 * at + 1 - core
        zs = at // nx
        kv_wait(theirs)
        dk, dv = block(full_slot, 2, kv_all[theirs, 0], kv_all[theirs, 1], None)
        part[theirs, 0] = dk.astype(bf16)
        part[theirs, 1] = dv.astype(bf16)
        spart_copy(at).start()
        dk, dv = block(full_slot, 2, kv_all[mine, 0], kv_all[mine, 1], None)
        pown[at, 0] = dk
        pown[at, 1] = dv

        @pl.when(t > 1)
        def _():
            combine(at + 1)

        @pl.when((lax.rem(at, nx) == 0) & (zs + 1 < z))
        def _():
            hop(zs + 1)

        @pl.when((lax.rem(at, nx) == 0) & (zs + 2 < z))
        def _():
            gather_x(zs + 2)

    loop(1, chip + 1, step)

    dq_full[...] = query_grads(2)
    back_q = remote(dq_full, dq_home, swap_send.at[6], swap_recv.at[6], me, pg)
    back_q.start()
    @pl.when(chip > 0)
    def _():
        combine(0)

    @pl.when(z > 0)
    def _():
        hop(0)

    @pl.when(z > 1)
    def _():
        gather_x(1)

    @pl.when(z > 0)
    def _():
        gather_x(0)

    @pl.when(core == 0)
    def _():
        sgrad_add(0)

        @pl.when(x > 0)
        def _():
            sgrad_send(x, at_place(z, 0, 0))

    @pl.when((x == 0) & (core == 0))
    def _():
        loop(1, nx, sgrad_add)

        @pl.when(z > 0)
        def _():
            sgrad_send(nx + z, 0)

    dq_near[...] = jnp.where(first_ret, dq_full[...], dq_band[0])
    out_near = pltpu.make_async_copy(dq_near, dq_out.at[:, 0], local_sem.at[0])
    out_near.start()

    @pl.when(me < n - 1)
    def _():
        back_copy.wait_recv()
        dkv_band[...] += back_recv[...].astype(f32)

    @pl.when(me == 0)
    def _():
        loop(1, nz, lambda zs: sgrad_add(nx + zs))
        dkv_band[:, :, 0:SINK] += sink_sum[...]

    @pl.when(core == 0)
    def _():
        sib_copy(me).wait_recv()
        dkv_own[...] += sib_part[...].astype(f32)

    def take_x(xs):
        x_copy(z, xs, x).wait_recv()
        dkv_own[...] += x_part[z, xs].astype(f32)

    loop(x + 1, nx, take_x)

    def take_z(zs):
        z_copy(zs, zs).wait_recv()
        dkv_own[...] += z_part[zs].astype(f32)

    loop(z + 1, nz, take_z)

    dkv_full[...] = dkv_own[...].astype(bf16)
    back_kv = remote(dkv_full, dkv_home, swap_send.at[8], swap_recv.at[8], me, pg)
    back_kv.start()
    dkv_out[0] = jnp.where(first_ret, dkv_full[...], dkv_band[0].astype(bf16))

    back_q.wait()
    dq_home[...] = jnp.where(second_ret, jnp.where(pair, dq_full[...], dq_home[...]), dq_band[1])
    out_far = pltpu.make_async_copy(dq_home, dq_out.at[:, 1], local_sem.at[1])
    out_far.start()
    back_kv.wait()
    dkv_out[1] = jnp.where(
        second_ret, jnp.where(pair, dkv_full[...], dkv_home[...]), dkv_band[1].astype(bf16)
    )

    for c in swaps:
        c.wait_send()

    loop(z + 1, nz, lambda zd: to_z(zd).wait_send())
    loop(x + 1, nx, lambda xd: to_x(z, xd).wait_send())

    def drain_z(zs):
        if nx == 4:
            to_x(zs, lax.rem(x + 1, nx)).wait_send()
            to_x(zs, lax.rem(x + nx - 1, nx)).wait_send()
            relay(zs).wait_send()
        else:
            for d in range(1, nx):
                to_x(zs, lax.rem(x + d, nx)).wait_send()

    loop(0, z, drain_z)
    loop(0, chip + 1 - core, lambda at: to_sib(at).wait_send())
    loop(0, 2 * chip + core, lambda blk: sib_copy(blk).wait_send())

    @pl.when(me < n - 1)
    def _():
        halo_copy.wait_send()

    @pl.when(me > 0)
    def _():
        back_copy.wait_send()
        sgrad_copy(0, sib).wait_send()

    @pl.when(me == 0)
    def _():
        loop(1, nz, lambda zd: sink_z(zd).wait_send())

    @pl.when((x == 0) & (core == 0))
    def _():
        loop(1, nx, lambda xd: sink_x(xd).wait_send())

    @pl.when(core == 0)
    def _():
        sink_copy(sib, sink_fs).wait_send()

    out_near.wait()
    out_far.wait()


def shards(queries, keys, values, outputs, grads, logs, kind, sinks, windows):
    tok, _, heads, hd = queries.shape
    rows = tok * heads
    n = lax.axis_size("ctx")
    nx = min(4, n // 2)
    nz = n // 2 // nx
    delta = jnp.sum(grads.astype(f32) * outputs.astype(f32), axis=-1)
    lse = logs.astype(f32) * LOG2E
    aux = jnp.stack([lse, delta], axis=0)
    aux = jnp.moveaxis(aux, 2, 0).reshape(2, 2, tok * heads)
    kv = jnp.moveaxis(jnp.stack([keys, values], axis=0), 2, 0)
    smem = pl.BlockSpec(memory_space=pltpu.SMEM)
    hbm = pl.BlockSpec(memory_space=pl.ANY)
    vmem = pl.BlockSpec(memory_space=pltpu.VMEM)
    V = pltpu.VMEM
    dma = pltpu.SemaphoreType.DMA
    dq, dkv = pl.pallas_call(
        functools.partial(kernel, n),
        in_specs=[smem, smem, smem, hbm, hbm, hbm, hbm],
        out_specs=[hbm, vmem],
        out_shape=[
            jax.ShapeDtypeStruct((tok, 2, heads, hd), bf16),
            jax.ShapeDtypeStruct((2, 2, tok, hd), bf16),
        ],
        scratch_shapes=[
            V((3, tok, heads, hd), bf16),
            V((3, tok, heads, hd), bf16),
            V((3, 2, tok, hd), bf16),
            V((3, 2, tok * heads), f32),
            V((n, 2, tok, hd), bf16),
            V((n // 2, 2, tok, hd), f32),
            V((n, 2, tok, hd), bf16),
            V((nz, nx, 2, tok, hd), bf16),
            V((nz, 2, tok, hd), bf16),
            V((nz, 2, tok, hd), bf16),
            V((2, tok, hd), bf16),
            V((n // 2, 2, tok, hd), bf16),
            V((2, 2, tok, hd), bf16),
            V((2, 2, SINK, hd), bf16),
            V((2, 2, SINK, hd), f32),
            V((2, 2, SINK, hd), bf16),
            V((nx + nz, 2, 2, SINK, hd), bf16),
            V((2, 2, tok, hd), bf16),
            V((2, 2, tok, hd), bf16),
            V((3, hd, rows), bf16),
            V((3, hd, rows), bf16),
            V((3, rows, hd), bf16),
            V((3, rows, hd), bf16),
            V((3, hd, rows), f32),
            V((2, tok, heads, hd), bf16),
            V((tok, heads, hd), bf16),
            V((tok, heads, hd), bf16),
            V((tok, heads, hd), bf16),
            V((2, tok, hd), f32),
            V((2, 2, tok, hd), f32),
            V((2, tok, hd), bf16),
            V((2, tok, hd), bf16),
            dma((12,)),
            dma((9,)),
            dma((9,)),
            dma((n,)),
            dma((nz,)),
            dma((nz, nx)),
            dma((nz,)),
            dma((n // 2,)),
            dma((n,)),
            dma((nz, nx)),
            dma((nz,)),
            dma((nz,)),
            dma,
            dma((n // 2,)),
            dma((nz,)),
            dma((nx,)),
            dma,
            dma,
            dma,
            dma((nx + nz,)),
            dma((4,)),
        ],
        compiler_params=pltpu.CompilerParams(
            collective_id=0, has_side_effects=True, vmem_limit_bytes=60 * 2**20
        ),
        name="attention_grads",
    )(kind, sinks, windows, queries, kv, grads, aux)
    dkv = jnp.moveaxis(dkv, 0, 2)
    return dq, dkv[0], dkv[1]


def solution(mesh):
    return jax.shard_map(
        shards,
        mesh=mesh,
        in_specs=(
            P("ctx", "hg", None, None),
            P("ctx", "hg", None),
            P("ctx", "hg", None),
            P("ctx", "hg", None, None),
            P("ctx", "hg", None, None),
            P("ctx", "hg", None),
            P(),
            P(),
            P(),
        ),
        out_specs=(P("ctx", "hg", None, None), P("ctx", "hg", None), P("ctx", "hg", None)),
        check_vma=False,
    )
```

time: 136 us -> 114 us (0.84)
  Pallas kernels: 127 us -> 105 us
    pallas_call x1, Pallas kernels: 127 us -> 105 us  [shards(): pl.pallas_call(functools.partial(kernel, n), in_specs=[smem, smem, smem,...]
where the time goes in v3:
time: 114 us
  Pallas kernels  105 us (92%)
  local copies, waits for them, and re-layouts  4.88 us (4%)
  other arithmetic  3.8 us (3%)
    pallas_call x1, Pallas kernels, shards(): pl.pallas_call(functools.partial(kernel, n), in_specs=[smem, smem, smem,...  105 us
    unnamed x9, local copies, waits for them, and re-layouts  2.57 us
    reduce_sum x1, other arithmetic, shards(): delta = jnp.sum(grads.astype(f32) * outputs.astype(f32), axis=-1)  2.36 us

profile of v3, /device:TPU:0, one launch (start us, length us, event | category | flops | bytes accessed | tf_op | source)
XLA Modules:
  0.0 113.9 jit_solution(3325078984946675177)
XLA Ops:
  0.6 0.7 multiply_bitcast_fusion
  1.3 0.0 copy-start.1
  1.3 0.0 copy-start.2
  1.3 2.4 %multiply_reduce_fusion = f32[256,2,8]{2,1,0:T(2,128)S(1)} fusion(bf16[256,2,8,128]{3,2,1,0:T(8,128)(2,1)} %param.12, bf16[256,2,8,128]{3,2,1,0:T(8,128)(2,1)} %do_in.1), kind=kLoop, calls=%fused_computation | loop fusion | flops 2093056 | bytes 2113536 | tf_op jit(solution)/shard_map/reduce_sum | solution.py:592
  3.7 0.1 copy.30
  3.8 0.0 copy-done.1
  3.8 0.0 copy-done.2
  3.9 0.7 maximum_bitcast_fusion.kv_in
  4.6 0.2 copy.31
  4.8 0.9 reshape.9.aux_in
  5.7 104.5 %attention_grads.1 = (bf16[256,2,8,128]{3,2,1,0:T(8,128)(2,1)}, bf16[2,2,256,128]{3,2,1,0:T(8,128)(2,1)}) custom-call(s32[8]{0:T(128)} %kind.1, s32[8]{0:T(128)} %sinks.1, s32[8]{0:T(128)} %windows.1, bf16[256,2,8,128]{3,2,1,0:T(8,128)(2,1)} %q_in.1, bf16[2,2,256,128]{3,2,1,0:T(8,128)(2,1)} %maximum_bitcast_fusion.kv_in, bf16[256,2,8,128]{3,2,1,0:T(8,128)(2,1)} %do_in.1, ...), custom_call_target="tpu_custom_call" | custom-call | tf_op jit(solution)/shard_map/attention_grads/pallas_call | solution.py:602
  110.3 0.0 copy-start
  110.3 1.1 slice_bitcast_fusion
  111.4 0.8 copy.33
  112.2 0.8 copy.32
  112.9 0.0 copy-done
  112.9 1.0 copy.37
  (2 shorter events, 0.0 us)
Async XLA Ops:
  1.3 2.5 %copy-start.1 = (bf16[256,2,128]{2,1,0:T(2,128)(2,1)S(1)}, bf16[256,2,128]{2,1,0:T(2,128)(2,1)}, u32[]{:S(2)}) copy-start(bf16[256,2,128]{2,1,0:T(2,128)(2,1)} %param.11) | copy-start | bytes 393220
  1.3 2.5 %copy-start.2 = (bf16[256,2,128]{2,1,0:T(2,128)(2,1)S(1)}, bf16[256,2,128]{2,1,0:T(2,128)(2,1)}, u32[]{:S(2)}) copy-start(bf16[256,2,128]{2,1,0:T(2,128)(2,1)} %param.10) | copy-start | bytes 393220
  110.3 2.7 %copy-start = (bf16[256,2,8,128]{3,2,1,0:T(8,128)(2,1)S(1)}, bf16[256,2,8,128]{3,2,1,0:T(8,128)(2,1)}, u32[]{:S(2)}) copy-start(bf16[256,2,8,128]{3,2,1,0:T(8,128)(2,1)} %get-tuple-element.26) | copy-start | bytes 3145732

commit v4 on v3

--- a/solution.py
+++ b/solution.py
@@ -26,13 +26,16 @@
     q_in,
     kv_in,
     do_in,
-    aux_in,
+    o_in,
+    lse_in,
     dq_out,
     dkv_out,
     q3,
     do3,
     kv3,
-    aux3,
+    o2,
+    lse3,
+    delta3,
     kv_all,
     pown,
     part,
@@ -124,7 +127,8 @@
         local.append((kv_in.at[slot], kv3.at[slot]))
         local.append((q_in.at[:, slot], q3.at[slot]))
         local.append((do_in.at[:, slot], do3.at[slot]))
-        local.append((aux_in.at[slot], aux3.at[slot]))
+        local.append((o_in.at[:, slot], o2.at[slot]))
+        local.append((lse_in.at[slot], lse3.at[slot]))
     local = [pltpu.make_async_copy(a, b, local_sem.at[i]) for i, (a, b) in enumerate(local)]
     for c in local:
         c.start()
@@ -145,7 +149,7 @@
 
     pieces = [
         (kv_in.at[1], kv3.at[2]),
-        (aux_in.at[1], aux3.at[2]),
+        (lse_in.at[1], lse3.at[2]),
         (q_in.at[:, 1], q3.at[2]),
         (do_in.at[:, 1], do3.at[2]),
     ]
@@ -211,13 +215,17 @@
         do_t[slot] = d.T
         dq_t[slot] = jnp.zeros((hd, rows), f32)
 
+    def row_totals(slot):
+        o_t = o2[slot].reshape(rows, hd).T.astype(f32)
+        delta3[slot] = jnp.sum(o_t * do_t[slot].astype(f32), axis=0, keepdims=True)
+
     def block(slot, acc, k, v, allowed):
         s = dot(k, q_t[slot])
-        p = jnp.exp2(s * (scale * LOG2E) - aux3[slot, 0:1, :])
+        p = jnp.exp2(s * (scale * LOG2E) - lse3[slot])
         if allowed is not None:
             p = jnp.where(allowed, p, 0.0)
         dp = dot(v, do_t[slot])
-        ds = (p * (dp - aux3[slot, 1:2, :])).astype(bf16)
+        ds = (p * (dp - delta3[slot])).astype(bf16)
         dv = dot(p.astype(bf16), do_r[slot])
         dk = dot(ds, q_r[slot])
         dq_t[acc] += dot(k.T, ds)
@@ -258,8 +266,12 @@
         sink_sum[slot, 1] = dv
         dq_band[slot] = query_grads(slot)
 
+    load_head(1)
+    row_totals(1)
+    delta_copy = remote(delta3.at[1], delta3.at[2], swap_send.at[4], swap_recv.at[4], me, pg)
+    delta_copy.start()
     load_head(0)
-    load_head(1)
+    row_totals(0)
     swaps[0].wait_recv()
     kv_all[me] = kv3[full_slot]
     loop(z + 1, nz, lambda zd: to_z(zd).start())
@@ -297,8 +309,6 @@
         if nx == 4:
             arrive(zs, lax.rem(x + 2, nx))
 
-    loop(1, z + 1, arrive_z)
-
     @pl.when((x == 0) & (core == 0))
     def _():
         @pl.when(z > 0)
@@ -307,20 +317,20 @@
 
         loop(1, nx, lambda xd: sink_x(xd).start())
 
+    loop(1, z + 1, arrive_z)
+
+    @pl.when((x > 0) & (core == 0))
+    def _():
+        sink_copy(sib, sink_fs).wait_recv()
+
+    @pl.when(core == 0)
+    def _():
+        sink_copy(sib, sink_fs).start()
+
     band(0)
     loop(0, x, lambda xs: arrive(z, xs))
+    band(1)
     loop(1, z + 1, lambda i: near(z - i))
-
-    @pl.when((x > 0) & (core == 0))
-    def _():
-        sink_copy(sib, sink_fs).wait_recv()
-
-    @pl.when(core == 0)
-    def _():
-        sink_copy(sib, sink_fs).start()
-
-    band(1)
-    loop(1, z + 1, lambda i: far(z - i))
 
     @pl.when(core == 1)
     def _():
@@ -328,6 +338,7 @@
 
     band_sink(0)
     band_sink(1)
+    loop(1, z + 1, lambda i: far(z - i))
 
     back_copy = remote(back_send, back_recv, edge_sem.at[2], edge_sem.at[3], before, g)
 
@@ -418,21 +429,9 @@
 
     for c in swaps[1:]:
         c.wait_recv()
+    delta_copy.wait_recv()
     load_head(2)
-    dk, dv = block(full_slot, 2, kv_all[me, 0], kv_all[me, 1], gap(tok, 0) >= 0)
-    dkv_own[0] = dk
-    dkv_own[1] = dv
-
-    @pl.when(core == 1)
-    def _():
-        kv_wait(sib)
-        dk, dv = block(full_slot, 2, kv_all[sib, 0], kv_all[sib, 1], None)
-        part[sib, 0] = dk.astype(bf16)
-        part[sib, 1] = dv.astype(bf16)
-        sib_copy(sib).start()
-
-    def step(t):
-        at = chip - t
+    def step(at):
         mine = 2 * at + core
         theirs = 2 * at + 1 - core
         zs = at // nx
@@ -445,38 +444,57 @@
         pown[at, 0] = dk
         pown[at, 1] = dv
 
-        @pl.when(t > 1)
+        @pl.when(at > 0)
         def _():
-            combine(at + 1)
-
-        @pl.when((lax.rem(at, nx) == 0) & (zs + 1 < z))
+            combine(at - 1)
+
+        @pl.when((lax.rem(at, nx) == 0) & (zs > 0))
         def _():
-            hop(zs + 1)
-
-        @pl.when((lax.rem(at, nx) == 0) & (zs + 2 < z))
+            hop(zs - 1)
+
+        @pl.when((lax.rem(at, nx) == 0) & (zs > 1))
         def _():
-            gather_x(zs + 2)
-
-    loop(1, chip + 1, step)
-
-    dq_full[...] = query_grads(2)
-    back_q = remote(dq_full, dq_home, swap_send.at[6], swap_recv.at[6], me, pg)
-    back_q.start()
+            gather_x(zs - 2)
+
+    loop(0, chip, step)
+
+    @pl.when(core == 1)
+    def _():
+        kv_wait(sib)
+        dk, dv = block(full_slot, 2, kv_all[sib, 0], kv_all[sib, 1], None)
+        part[sib, 0] = dk.astype(bf16)
+        part[sib, 1] = dv.astype(bf16)
+        sib_copy(sib).start()
+
     @pl.when(chip > 0)
     def _():
-        combine(0)
+        combine(chip - 1)
+
+    @pl.when((z > 0) & (x == 0))
+    def _():
+        hop(z - 1)
+
+    @pl.when((z > 1) & (x == 0))
+    def _():
+        gather_x(z - 2)
 
     @pl.when(z > 0)
     def _():
-        hop(0)
-
-    @pl.when(z > 1)
-    def _():
-        gather_x(1)
-
-    @pl.when(z > 0)
-    def _():
-        gather_x(0)
+        gather_x(z - 1)
+
+    dk, dv = block(full_slot, 2, kv_all[me, 0], kv_all[me, 1], gap(tok, 0) >= 0)
+    dkv_own[0] = dk
+    dkv_own[1] = dv
+
+
+    back_q = []
+    for i in range(2):
+        here = pl.ds(i * (tok // 2), tok // 2)
+        grads = dq_t[2, :, i * (rows // 2) : (i + 1) * (rows // 2)] * scale
+        dq_full[here] = grads.T.astype(bf16).reshape(tok // 2, heads, hd)
+        c = remote(dq_full.at[here], dq_home.at[here], swap_send.at[5 + i], swap_recv.at[5 + i], me, pg)
+        c.start()
+        back_q.append(c)
 
     @pl.when(core == 0)
     def _():
@@ -530,10 +548,15 @@
     back_kv.start()
     dkv_out[0] = jnp.where(first_ret, dkv_full[...], dkv_band[0].astype(bf16))
 
-    back_q.wait()
-    dq_home[...] = jnp.where(second_ret, jnp.where(pair, dq_full[...], dq_home[...]), dq_band[1])
-    out_far = pltpu.make_async_copy(dq_home, dq_out.at[:, 1], local_sem.at[1])
-    out_far.start()
+    out_far = []
+    for i in range(2):
+        here = pl.ds(i * (tok // 2), tok // 2)
+        back_q[i].wait()
+        home = jnp.where(pair, dq_full[here], dq_home[here])
+        dq_home[here] = jnp.where(second_ret, home, dq_band[1, here])
+        c = pltpu.make_async_copy(dq_home.at[here], dq_out.at[here, 1], local_sem.at[1 + i])
+        c.start()
+        out_far.append(c)
     back_kv.wait()
     dkv_out[1] = jnp.where(
         second_ret, jnp.where(pair, dkv_full[...], dkv_home[...]), dkv_band[1].astype(bf16)
@@ -541,6 +564,7 @@
 
     for c in swaps:
         c.wait_send()
+    delta_copy.wait_send()
 
     loop(z + 1, nz, lambda zd: to_z(zd).wait_send())
     loop(x + 1, nx, lambda xd: to_x(z, xd).wait_send())
@@ -580,7 +604,8 @@
         sink_copy(sib, sink_fs).wait_send()
 
     out_near.wait()
-    out_far.wait()
+    for c in out_far:
+        c.wait()
 
 
 def shards(queries, keys, values, outputs, grads, logs, kind, sinks, windows):
@@ -589,10 +614,7 @@
     n = lax.axis_size("ctx")
     nx = min(4, n // 2)
     nz = n // 2 // nx
-    delta = jnp.sum(grads.astype(f32) * outputs.astype(f32), axis=-1)
-    lse = logs.astype(f32) * LOG2E
-    aux = jnp.stack([lse, delta], axis=0)
-    aux = jnp.moveaxis(aux, 2, 0).reshape(2, 2, tok * heads)
+    lse = jnp.moveaxis(logs.astype(f32) * LOG2E, 1, 0).reshape(2, 1, rows)
     kv = jnp.moveaxis(jnp.stack([keys, values], axis=0), 2, 0)
     smem = pl.BlockSpec(memory_space=pltpu.SMEM)
     hbm = pl.BlockSpec(memory_space=pl.ANY)
@@ -601,7 +623,7 @@
     dma = pltpu.SemaphoreType.DMA
     dq, dkv = pl.pallas_call(
         functools.partial(kernel, n),
-        in_specs=[smem, smem, smem, hbm, hbm, hbm, hbm],
+        in_specs=[smem, smem, smem, hbm, hbm, hbm, hbm, hbm],
         out_specs=[hbm, vmem],
         out_shape=[
             jax.ShapeDtypeStruct((tok, 2, heads, hd), bf16),
@@ -611,7 +633,9 @@
             V((3, tok, heads, hd), bf16),
             V((3, tok, heads, hd), bf16),
             V((3, 2, tok, hd), bf16),
-            V((3, 2, tok * heads), f32),
+            V((2, tok, heads, hd), bf16),
+            V((3, 1, rows), f32),
+            V((3, 1, rows), f32),
             V((n, 2, tok, hd), bf16),
             V((n // 2, 2, tok, hd), f32),
             V((n, 2, tok, hd), bf16),
@@ -640,7 +664,7 @@
             V((2, 2, tok, hd), f32),
             V((2, tok, hd), bf16),
             V((2, tok, hd), bf16),
-            dma((12,)),
+            dma((10,)),
             dma((9,)),
             dma((9,)),
             dma((n,)),
@@ -666,7 +690,7 @@
             collective_id=0, has_side_effects=True, vmem_limit_bytes=60 * 2**20
         ),
         name="attention_grads",
-    )(kind, sinks, windows, queries, kv, grads, aux)
+    )(kind, sinks, windows, queries, kv, grads, outputs, lse)
     dkv = jnp.moveaxis(dkv, 0, 2)
     return dq, dkv[0], dkv[1]
 

time: 114 us -> 108 us (0.947)
  Pallas kernels: 105 us -> 101 us
  other arithmetic: 3.8 us -> 1.43 us
    pallas_call x1, Pallas kernels: 105 us -> 101 us  [shards(): pl.pallas_call(functools.partial(kernel, n), in_specs=[smem, smem, smem,...]
    reduce_sum x1 -> x0, other arithmetic: 2.36 us -> none  [shards(): delta = jnp.sum(grads.astype(f32) * outputs.astype(f32), axis=-1)]
where the time goes in v4:
time: 108 us
  Pallas kernels  101 us (94%)
  local copies, waits for them, and re-layouts  4.75 us (4%)
  other arithmetic  1.43 us (1%)
    pallas_call x1, Pallas kernels, shards(): pl.pallas_call(functools.partial(kernel, n), in_specs=[smem, smem, smem,...  101 us
    unnamed x9, local copies, waits for them, and re-layouts  2.74 us

profile of v4, /device:TPU:0, one launch (start us, length us, event | category | flops | bytes accessed | tf_op | source)
XLA Modules:
  0.0 107.7 jit_solution(6585727629783899255)
XLA Ops:
  0.6 0.7 multiply_bitcast_fusion
  1.3 0.1 copy.19
  1.5 0.0 copy-start.1
  1.5 0.0 copy-start.2
  1.5 0.8 reshape.10.lse_in
  2.3 0.1 copy-done.1
  2.4 0.1 copy-done.2
  2.5 0.7 maximum_bitcast_fusion.kv_in
  3.2 100.8 %attention_grads.1 = (bf16[256,2,8,128]{3,2,1,0:T(8,128)(2,1)}, bf16[2,2,256,128]{3,2,1,0:T(8,128)(2,1)}) custom-call(s32[8]{0:T(128)} %kind.1, s32[8]{0:T(128)} %sinks.1, s32[8]{0:T(128)} %windows.1, bf16[256,2,8,128]{3,2,1,0:T(8,128)(2,1)} %q_in.1, bf16[2,2,256,128]{3,2,1,0:T(8,128)(2,1)} %maximum_bitcast_fusion.kv_in, bf16[256,2,8,128]{3,2,1,0:T(8,128)(2,1)} %do_in.1, ...), custom_call_target="tpu_custom_call" | custom-call | tf_op jit(solution)/shard_map/attention_grads/pallas_call | solution.py:624
  104.0 0.0 copy-start
  104.0 1.1 %slice_bitcast_fusion = (bf16[256,2,128]{2,0,1:T(8,128)(2,1)S(1)}, bf16[256,2,128]{2,0,1:T(8,128)(2,1)S(1)}) fusion(bf16[2,256,2,128]{3,1,0,2:T(8,128)(2,1)} %bitcast.13), kind=kLoop, calls=%fused_computation.1 | loop fusion | bytes 524288 | tf_op jit(solution)/shard_map/squeeze | solution.py:695
  105.1 0.8 copy.22
  105.9 0.8 copy.21
  106.7 0.0 copy-done
  106.7 1.0 copy.26
  (1 shorter events, 0.0 us)
Async XLA Ops:
  1.5 0.9 copy-start.1
  1.5 1.0 copy-start.2
  104.0 2.7 %copy-start = (bf16[256,2,8,128]{3,2,1,0:T(8,128)(2,1)S(1)}, bf16[256,2,8,128]{3,2,1,0:T(8,128)(2,1)}, u32[]{:S(2)}) copy-start(bf16[256,2,8,128]{3,2,1,0:T(8,128)(2,1)} %get-tuple-element.20) | copy-start | bytes 3145732

commit v5 on v4

--- a/solution.py
+++ b/solution.py
@@ -154,8 +154,7 @@
         (do_in.at[:, 1], do3.at[2]),
     ]
     swaps = [remote(a, b, swap_send.at[i], swap_recv.at[i], me, pg) for i, (a, b) in enumerate(pieces)]
-    for c in swaps:
-        c.start()
+    swaps[0].start()
 
     kinds = [kind[2 * g], kind[2 * g + 1]]
     first_ret = kinds[0] == 1
@@ -273,6 +272,8 @@
     load_head(0)
     row_totals(0)
     swaps[0].wait_recv()
+    for c in swaps[1:]:
+        c.start()
     kv_all[me] = kv3[full_slot]
     loop(z + 1, nz, lambda zd: to_z(zd).start())
     loop(x + 1, nx, lambda xd: to_x(z, xd).start())
@@ -329,8 +330,9 @@
 
     band(0)
     loop(0, x, lambda xs: arrive(z, xs))
+    loop(1, z + 1, lambda i: near(z - i))
     band(1)
-    loop(1, z + 1, lambda i: near(z - i))
+    loop(1, z + 1, lambda i: far(z - i))
 
     @pl.when(core == 1)
     def _():
@@ -338,7 +340,6 @@
 
     band_sink(0)
     band_sink(1)
-    loop(1, z + 1, lambda i: far(z - i))
 
     back_copy = remote(back_send, back_recv, edge_sem.at[2], edge_sem.at[3], before, g)
 

time: 108 us -> 107 us (level)
  Pallas kernels: 101 us -> 99.6 us
    pallas_call x1, Pallas kernels: 101 us -> 99.6 us  [shards(): pl.pallas_call(functools.partial(kernel, n), in_specs=[smem, smem, smem,...]
where the time goes in v5:
time: 107 us; the launch traced here: 106 us
  Pallas kernels  99.6 us (93%)
  local copies, waits for them, and re-layouts  4.75 us (4%)
  other arithmetic  1.43 us (1%)
    pallas_call x1, Pallas kernels, shards(): pl.pallas_call(functools.partial(kernel, n), in_specs=[smem, smem, smem,...  99.6 us
    unnamed x9, local copies, waits for them, and re-layouts  2.74 us

profile of v5, /device:TPU:0, one launch (start us, length us, event | category | flops | bytes accessed | tf_op | source)
XLA Modules:
  0.0 106.4 jit_solution(9601598617611747144)
XLA Ops:
  0.6 0.7 multiply_bitcast_fusion
  1.3 0.1 copy.19
  1.5 0.0 copy-start.1
  1.5 0.0 copy-start.2
  1.5 0.8 reshape.10.lse_in
  2.3 0.1 copy-done.1
  2.4 0.1 copy-done.2
  2.5 0.7 maximum_bitcast_fusion.kv_in
  3.2 99.6 %attention_grads.1 = (bf16[256,2,8,128]{3,2,1,0:T(8,128)(2,1)}, bf16[2,2,256,128]{3,2,1,0:T(8,128)(2,1)}) custom-call(s32[8]{0:T(128)} %kind.1, s32[8]{0:T(128)} %sinks.1, s32[8]{0:T(128)} %windows.1, bf16[256,2,8,128]{3,2,1,0:T(8,128)(2,1)} %q_in.1, bf16[2,2,256,128]{3,2,1,0:T(8,128)(2,1)} %maximum_bitcast_fusion.kv_in, bf16[256,2,8,128]{3,2,1,0:T(8,128)(2,1)} %do_in.1, ...), custom_call_target="tpu_custom_call" | custom-call | tf_op jit(solution)/shard_map/attention_grads/pallas_call | solution.py:625
  102.8 0.0 copy-start
  102.8 1.1 %slice_bitcast_fusion = (bf16[256,2,128]{2,0,1:T(8,128)(2,1)S(1)}, bf16[256,2,128]{2,0,1:T(8,128)(2,1)S(1)}) fusion(bf16[2,256,2,128]{3,1,0,2:T(8,128)(2,1)} %bitcast.13), kind=kLoop, calls=%fused_computation.1 | loop fusion | bytes 524288 | tf_op jit(solution)/shard_map/squeeze | solution.py:696
  103.9 0.8 copy.22
  104.7 0.8 copy.21
  105.4 0.0 copy-done
  105.4 1.0 copy.26
  (1 shorter events, 0.0 us)
Async XLA Ops:
  1.5 0.9 copy-start.1
  1.5 1.0 copy-start.2
  102.8 2.7 %copy-start = (bf16[256,2,8,128]{3,2,1,0:T(8,128)(2,1)S(1)}, bf16[256,2,8,128]{3,2,1,0:T(8,128)(2,1)}, u32[]{:S(2)}) copy-start(bf16[256,2,8,128]{3,2,1,0:T(8,128)(2,1)} %get-tuple-element.20) | copy-start | bytes 3145732

commit v6 on v5

--- a/solution.py
+++ b/solution.py
@@ -433,17 +433,18 @@
     delta_copy.wait_recv()
     load_head(2)
     def step(at):
-        mine = 2 * at + core
         theirs = 2 * at + 1 - core
         zs = at // nx
         kv_wait(theirs)
-        dk, dv = block(full_slot, 2, kv_all[theirs, 0], kv_all[theirs, 1], None)
-        part[theirs, 0] = dk.astype(bf16)
-        part[theirs, 1] = dv.astype(bf16)
+        both = pl.ds(2 * at, 2)
+        keys = kv_all[both, 0].reshape(2 * tok, hd)
+        values = kv_all[both, 1].reshape(2 * tok, hd)
+        dk, dv = block(full_slot, 2, keys, values, None)
+        part[theirs, 0] = jnp.where(core == 0, dk[tok:], dk[:tok]).astype(bf16)
+        part[theirs, 1] = jnp.where(core == 0, dv[tok:], dv[:tok]).astype(bf16)
         spart_copy(at).start()
-        dk, dv = block(full_slot, 2, kv_all[mine, 0], kv_all[mine, 1], None)
-        pown[at, 0] = dk
-        pown[at, 1] = dv
+        pown[at, 0] = jnp.where(core == 0, dk[:tok], dk[tok:])
+        pown[at, 1] = jnp.where(core == 0, dv[:tok], dv[tok:])
 
         @pl.when(at > 0)
         def _():

time: 107 us -> 106 us (level)
  no operation moved by 1% of the time
where the time goes in v6:
time: 106 us
  Pallas kernels  99.4 us (94%)
  local copies, waits for them, and re-layouts  4.75 us (4%)
  other arithmetic  1.43 us (1%)
    pallas_call x1, Pallas kernels, shards(): pl.pallas_call(functools.partial(kernel, n), in_specs=[smem, smem, smem,...  99.4 us
    unnamed x9, local copies, waits for them, and re-layouts  2.74 us

profile of v6, /device:TPU:0, one launch (start us, length us, event | category | flops | bytes accessed | tf_op | source)
XLA Modules:
  0.0 106.3 jit_solution(8047694653376922713)
XLA Ops:
  0.6 0.7 multiply_bitcast_fusion
  1.3 0.1 copy.19
  1.5 0.0 copy-start.1
  1.5 0.0 copy-start.2
  1.5 0.8 reshape.10.lse_in
  2.3 0.1 copy-done.1
  2.4 0.1 copy-done.2
  2.5 0.7 maximum_bitcast_fusion.kv_in
  3.2 99.4 %attention_grads.1 = (bf16[256,2,8,128]{3,2,1,0:T(8,128)(2,1)}, bf16[2,2,256,128]{3,2,1,0:T(8,128)(2,1)}) custom-call(s32[8]{0:T(128)} %kind.1, s32[8]{0:T(128)} %sinks.1, s32[8]{0:T(128)} %windows.1, bf16[256,2,8,128]{3,2,1,0:T(8,128)(2,1)} %q_in.1, bf16[2,2,256,128]{3,2,1,0:T(8,128)(2,1)} %maximum_bitcast_fusion.kv_in, bf16[256,2,8,128]{3,2,1,0:T(8,128)(2,1)} %do_in.1, ...), custom_call_target="tpu_custom_call" | custom-call | tf_op jit(solution)/shard_map/attention_grads/pallas_call | solution.py:626
  102.6 0.0 copy-start
  102.7 1.1 %slice_bitcast_fusion = (bf16[256,2,128]{2,0,1:T(8,128)(2,1)S(1)}, bf16[256,2,128]{2,0,1:T(8,128)(2,1)S(1)}) fusion(bf16[2,256,2,128]{3,1,0,2:T(8,128)(2,1)} %bitcast.13), kind=kLoop, calls=%fused_computation.1 | loop fusion | bytes 524288 | tf_op jit(solution)/shard_map/squeeze | solution.py:697
  103.7 0.8 copy.22
  104.5 0.8 copy.21
  105.3 0.0 copy-done
  105.3 1.0 copy.26
  (1 shorter events, 0.0 us)
Async XLA Ops:
  1.5 0.9 copy-start.1
  1.5 1.0 copy-start.2
  102.6 2.7 %copy-start = (bf16[256,2,8,128]{3,2,1,0:T(8,128)(2,1)S(1)}, bf16[256,2,8,128]{3,2,1,0:T(8,128)(2,1)}, u32[]{:S(2)}) copy-start(bf16[256,2,8,128]{3,2,1,0:T(8,128)(2,1)} %get-tuple-element.20) | copy-start | bytes 3145732
